TPU v7x, 32 devices: a whole 2x2x4 slice. The times are simulated.
32 devices in a mesh: group: 2 (over x), dp: 16 (over z, y, core).
Axes of the slice: x: 2, y: 2, z: 4, core: 2. Of those that a mesh axis runs over, the one named last changes fastest.
Arguments:
- acts: bfloat16 [16384, 4096], P(('group', 'dp')), parts along dimension 0, may hold values from -120 to 120
- grad_q: bfloat16 [16384, 4096], P(('group', 'dp')), parts along dimension 0, may hold values from -120 to 120
- grad_k: bfloat16 [16384, 1024], P(('group', 'dp')), parts along dimension 0, may hold values from -120 to 120
- grad_v: bfloat16 [16384, 1024], P(('group', 'dp')), parts along dimension 0, may hold values from -120 to 120
- proj_in: bfloat16 [64, 4096], replicated, may hold values from -0.09375 to 0.09375
- proj_q: bfloat16 [64, 4096], replicated, may hold values from -0.09375 to 0.09375
- proj_k: bfloat16 [64, 1024], replicated, may hold values from -0.1875 to 0.1875
- proj_v: bfloat16 [64, 1024], replicated, may hold values from -0.1875 to 0.1875
- query_ids: int32 [32], P(('group', 'dp')), parts along dimension 0, may hold values from 0 to 3
Outputs:
- scores: float32 [128, 16], P(('group', 'dp')), parts along dimension 0
There are 2 independent parts, one for each index of `group`. A program takes and returns all parts, laid end to end along the dimension named above; an argument that names none is the same for every part. Nothing has to cross between parts.
Inputs may be any that keep to these rules, and one draw needn't show every extreme that they name: `query_ids`: each entry numbers a sequence from 0 within the 4 training sequences of the dp index that holds the entry.
All inputs are finite; a program needn't handle non-finite values.
Results may differ from a plain program's by a relative error of at most 0.0003.
Values sent between devices are 32-bit elements; how exact they have to be, the bound alone decides.
No kernel may reach another device: no remote copies, remote signals or barrier semaphores. Data moves between devices by JAX's collectives and lax.ppermute only.
A program may use at most 64 MiB of HBM per device.

v0:
```python
import functools

import jax
import jax.numpy as jnp
from jax import lax
from jax.experimental import pallas as pl
from jax.experimental.pallas import tpu as pltpu
from jax.sharding import PartitionSpec as P

LEN = 128
LANES = 128
PANEL = 8
HALF = 128
IN_FLIGHT = 6
MESSAGES = 4
HIGHEST = lax.Precision.HIGHEST
FRONT_VMEM_BYTES = 24 * 1024 * 1024
VMEM_BYTES = 8 * 1024 * 1024
NT = (((1,), (1,)), ((), ()))
TN = (((0,), (0,)), ((), ()))
NN = (((1,), (0,)), ((), ()))


def dot(a, b, dims, precision=HIGHEST):
    return lax.dot_general(a, b, dims, precision=precision, preferred_element_type=jnp.float32)


def places(order):
    shape = (order, 2 * order)
    lane = lax.broadcasted_iota(jnp.int32, shape, 1)
    return lax.broadcasted_iota(jnp.int32, shape, 0), lane % order


def dot_split(a, b, dims):
    a_high, b_high = a.astype(jnp.bfloat16), b.astype(jnp.bfloat16)
    a_low = (a - a_high.astype(jnp.float32)).astype(jnp.bfloat16)
    b_low = (b - b_high.astype(jnp.float32)).astype(jnp.bfloat16)
    return (
        dot(a_high, b_high, dims, None) + dot(a_low, b_high, dims, None) + dot(a_high, b_low, dims, None)
    )


def front_kernel(
    total_tokens, sequences, width,
    ids, acts, grad_q, grad_k, grad_v, proj_in, proj_q, proj_k, proj_v,
    factors, grams, query,
    acts_v, gq_v, gk_v, gv_v, pi_v, pq_v, pk_v, pv_v, sem,
):
    tokens = acts.shape[0]
    rows = min(HALF, tokens)
    moves = [(proj_k, pk_v), (grad_k, gk_v), (proj_v, pv_v), (grad_v, gv_v)]
    for first in range(0, tokens, rows):
        for src, dst, table, table_v in ((acts, acts_v, proj_in, pi_v), (grad_q, gq_v, proj_q, pq_v)):
            if first == 0:
                moves.append((table, table_v))
            box = pl.ds(first, rows)
            moves.append((src.at[box], dst.at[box]))
    copies = [pltpu.make_async_copy(src, dst, sem.at[i]) for i, (src, dst) in enumerate(moves)]
    for copy in copies[:IN_FLIGHT]:
        copy.start()
    waited = []

    def arrived(count):
        for _ in range(count):
            i = len(waited)
            copies[i].wait()
            if i + IN_FLIGHT < len(copies):
                copies[i + IN_FLIGHT].start()
            waited.append(i)

    left = lax.broadcasted_iota(jnp.int32, (width, 2 * width), 1) < width
    sums = [None, None]

    def gram_blocks(first, sides):
        coords = jnp.concatenate(sides, axis=0)
        high = coords.astype(jnp.bfloat16)
        low = (coords - high.astype(jnp.float32)).astype(jnp.bfloat16)
        for seq in range(rows // LEN):
            here = slice(seq * LEN, (seq + 1) * LEN)
            one = jnp.concatenate([high[:, here], low[:, here], high[:, here]], axis=1)
            other = jnp.concatenate([high[:, here], high[:, here], low[:, here]], axis=1)
            gram = dot(one, other, NT, None)
            grams[first // LEN + seq] = gram[:width] * (1.0 / LEN)
            squares = [gram[p * width : (p + 1) * width, p // 2 * 2 * width : (p // 2 + 1) * 2 * width] for p in range(4)]
            for i in range(2):
                pair = jnp.where(left, squares[2 * i], squares[2 * i + 1])
                sums[i] = pair if sums[i] is None else sums[i] + pair

    def projected(table, data, turned):
        return dot(data, table, NT, None).T if turned else dot(table, data, NT, None)

    arrived(4)
    coords_k = projected(pk_v[...], gk_v[...], False)
    coords_v = projected(pv_v[...], gv_v[...], True)
    ready = None
    for first in range(0, tokens, rows):
        whole = slice(first, first + rows)
        arrived(4 if first == 0 else 2)
        sides = [projected(pi_v[...], acts_v[whole], False), projected(pq_v[...], gq_v[whole], True)]
        if ready is not None:
            gram_blocks(*ready)
        ready = first, sides + [coords_k[:, whole], coords_v[:, whole]]
    gram_blocks(*ready)
    upper, lower = sums
    row, column = places(width)
    scale = 1.0 / total_tokens
    factors[:width] = jnp.where(column >= row, upper, lower) * scale
    diagonal = jnp.sum(jnp.where(column == row, lower, 0.0), axis=0, keepdims=True) * scale
    factors[width:] = jnp.broadcast_to(diagonal, (factors.shape[0] - width, 2 * width))
    half = width // 2
    for q in range(query.shape[0]):
        chosen = grams[ids[q]]
        query[q, :width] = chosen[:, 2 * width :]
        in_q = chosen[:, : 2 * width]
        query[q, width:] = jnp.where(left[:half], pltpu.roll(in_q[:half], width, 1), in_q[half:])


def damped(packed):
    order = packed.shape[1] // 2
    half = order // 2
    square, diagonal = packed[:order], packed[order : order + 1]
    row, column = places(order)
    turned = square.T
    turned = jnp.concatenate([turned[:order], turned[order:]], axis=1)
    on_diagonal = column == row
    first = jnp.where(column >= row, square, turned)
    second = jnp.where(column < row, square, turned)
    second = jnp.where(on_diagonal, diagonal, second)
    first_diagonal = jnp.sum(jnp.where(on_diagonal, square, 0.0), axis=0, keepdims=True)
    shape = (LANES, LANES)
    same = (
        lax.broadcasted_iota(jnp.int32, shape, 0) // order
        == lax.broadcasted_iota(jnp.int32, shape, 1) // order
    )
    diagonals = jnp.concatenate([first_diagonal, diagonal], axis=0)
    diagonals = jnp.concatenate([diagonals] * 4, axis=0)
    scales = 1.0 / dot(diagonals, jnp.where(same, 1.0 / order, 0.0), NN)
    damping = jnp.where(on_diagonal, 0.1, 0.0)
    first = first * scales[:1] + damping
    second = second * scales[1:2] + damping
    is_low = column < half
    low = jnp.where(is_low, first, pltpu.roll(second, half, 1))
    high = jnp.where(is_low, pltpu.roll(first, LANES - half, 1), second)
    scale = jnp.where(is_low[:8], spread_row(scales, 0), pltpu.roll(spread_row(scales, 1), half, 1))
    return low, high, scale


def spread_row(x, r):
    return jnp.broadcast_to(x[r : r + 1], x.shape)


def invert(low, high, scale):
    order = low.shape[0]
    half = order // 2
    groups = order // 8
    state = [[x[8 * g : 8 * g + 8] for g in range(groups)] for x in (low, high)]
    lane = lax.broadcasted_iota(jnp.int32, (8, LANES), 1)
    row = lax.broadcasted_iota(jnp.int32, (8, LANES), 0)
    column_of_lane = lane % half
    first_lane = lane - column_of_lane
    for start in range(0, order, PANEL):
        h, first = start // half, start % half
        spread = [
            [jnp.take_along_axis(state[h][g], first_lane + (first + j), axis=1) for g in range(groups)]
            for j in range(PANEL)
        ]
        in_panel = (column_of_lane >= first) & (column_of_lane < first + PANEL)
        state[h] = [jnp.where(in_panel, 0.0, x) for x in state[h]]
        for j in range(0, PANEL, 2):
            k = start + j
            g, r = k // 8, k % 8
            first_column, second_column = spread[j], spread[j + 1]
            a, c = spread_row(first_column[g], r), spread_row(first_column[g], r + 1)
            b, d = spread_row(second_column[g], r), spread_row(second_column[g], r + 1)
            inverse_det = 1.0 / (a * d - b * c)

            def eliminate(x, unit=None):
                top, bottom = spread_row(x[g], r), spread_row(x[g], r + 1)
                if unit is not None:
                    top = jnp.where(column_of_lane == unit, 1.0, top)
                    bottom = jnp.where(column_of_lane == unit + 1, 1.0, bottom)
                one, two = (d * top - b * bottom) * inverse_det, (a * bottom - c * top) * inverse_det
                done = [x[i] - first_column[i] * one - second_column[i] * two for i in range(groups)]
                done[g] = jnp.where(row == r, one, jnp.where(row == r + 1, two, done[g]))
                return done

            state = [eliminate(state[t], first + j if t == h else None) for t in range(2)]
            for i in range(j + 2, PANEL):
                spread[i] = eliminate(spread[i])
    return [jnp.concatenate([x * scale for x in half_state], axis=0) for half_state in state]


def invert_kernel(sequences, width, first, second, grams, train, side_v, left_v):
    half = width // 2
    low, high = invert(*damped(first[...] + second[...]))
    by_lanes = [
        jnp.concatenate([low[:, p * half : (p + 1) * half], high[:, p * half : (p + 1) * half]], axis=1)
        for p in range(4)
    ]
    inverse_in, inverse_k, inverse_q, inverse_v = by_lanes
    side_v[...] = jnp.zeros_like(side_v)
    side_v[width : 2 * width, 2 * width : 3 * width] = inverse_q
    side_v[width : 2 * width, 3 * width :] = inverse_q
    side_v[2 * width : 3 * width, :width] = inverse_k
    side_v[3 * width :, width : 2 * width] = inverse_v
    left_v[...] = dot_split(grams[...].reshape(sequences * width, 4 * width), side_v[...], NN)
    on_left = lax.broadcasted_iota(jnp.int32, (half, 2 * width), 1) < width
    for s in range(sequences):
        done = dot_split(inverse_in, left_v[pl.ds(s * width, width)], NN)
        train[s, :width] = done[:, : 2 * width]
        train[s, width:] = jnp.where(on_left, done[:half, 2 * width :], done[half:, 2 * width :])


def score_kernel(offsets, own, train, *refs):
    blocks, out, partial = refs[:-2], refs[-2], refs[-1]
    me = lax.axis_index("dp")
    slot = 0
    for block in blocks:
        for i in range(block.shape[0]):
            value = block[i]
            place = ((me ^ offsets[slot // own]) * own + slot % own) * 8
            for s in range(train.shape[0]):
                product = (train[s] * value).reshape(-1, 8, train.shape[2])
                partial[s, pl.ds(pl.multiple_of(place, 8), 8)] = jnp.sum(product, axis=0)
            slot += 1
    ones = jnp.ones((8, train.shape[2]), jnp.float32)
    for s in range(train.shape[0]):
        by_query = jnp.sum(partial[s].reshape(-1, 8, train.shape[2]), axis=1)
        out[pl.ds(s, 1)] = dot(ones, by_query, NT)[:1]


def exchange(x, devices, distance):
    return lax.ppermute(x, "dp", [(i, i ^ distance) for i in range(devices)])


def per_device(acts, grad_q, grad_k, grad_v, proj_in, proj_q, proj_k, proj_v, query_ids):
    devices = lax.axis_size("dp")
    steps = devices.bit_length() - 1
    tokens, width = acts.shape[0], proj_in.shape[0]
    sequences, own_queries = tokens // LEN, query_ids.shape[0]
    queries = own_queries * devices
    f32 = jnp.float32
    in_vmem = pl.BlockSpec(memory_space=pltpu.VMEM)
    in_hbm = pl.BlockSpec(memory_space=pltpu.HBM)
    params = pltpu.CompilerParams(vmem_limit_bytes=VMEM_BYTES)
    tables = tuple(
        pltpu.with_memory_space_constraint(t, pltpu.HBM)
        for t in (acts, grad_q, grad_k, grad_v, proj_in, proj_q, proj_k, proj_v)
    )

    factors, grams, query = pl.pallas_call(
        functools.partial(front_kernel, tokens * devices, sequences, width),
        out_shape=(
            jax.ShapeDtypeStruct((width + 8, 2 * width), f32),
            jax.ShapeDtypeStruct((sequences, width, 4 * width), f32),
            jax.ShapeDtypeStruct((own_queries, 3 * width // 2, 2 * width), f32),
        ),
        in_specs=[pl.BlockSpec(memory_space=pltpu.SMEM)] + [in_hbm] * 8,
        out_specs=(in_vmem,) * 3,
        scratch_shapes=[pltpu.VMEM(t.shape, t.dtype) for t in tables]
        + [pltpu.SemaphoreType.DMA((6 + 2 * -(-tokens // HALF),))],
        compiler_params=pltpu.CompilerParams(vmem_limit_bytes=FRONT_VMEM_BYTES),
        name="front",
    )(query_ids, *tables)

    factor_bits = list(range(steps))
    if steps > 2:
        factor_bits[1], factor_bits[2] = 2, 1
    query_bits = list(range(1, steps))[::-1]

    def send(items, bit):
        size = -(-len(items) // MESSAGES)
        groups = [items[i : i + size] for i in range(0, len(items), size)]
        return [
            (
                exchange(jnp.concatenate([x for x, _ in group], axis=0) if size > 1 else group[0][0], devices, 1 << bit),
                [offset ^ 1 << bit for _, offsets in group for offset in offsets],
            )
            for group in groups
        ]

    def after(items, token):
        arrays = lax.optimization_barrier((*[x for x, _ in items], token))[:-1]
        return [(x, offsets) for x, (_, offsets) in zip(arrays, items)]

    own = [(query, [0])]
    mine, blocks, pending, early = factors, [], [], []
    for step in range(steps):
        theirs = exchange(mine, devices, 1 << factor_bits[step])
        if step == 0:
            pending = send(own, query_bits[0])
        elif step == 1:
            early = send(after(own, mine), query_bits[-1])
        else:
            blocks += after(pending, mine)
            last = step == steps - 1
            pending = send(([] if last else after(own, mine)) + blocks, query_bits[step - 1])
        if step < steps - 1:
            mine = mine + theirs
    terms = (mine, theirs)
    train = pl.pallas_call(
        functools.partial(invert_kernel, sequences, width),
        out_shape=jax.ShapeDtypeStruct((sequences, 3 * width // 2, 2 * width), f32),
        in_specs=[in_vmem] * 3,
        out_specs=in_vmem,
        scratch_shapes=[
            pltpu.VMEM((4 * width, 4 * width), f32),
            pltpu.VMEM((sequences * width, 4 * width), f32),
        ],
        compiler_params=params,
        name="invert",
    )(*terms, grams)
    blocks = own + blocks + after(pending + early, train)
    everything = jnp.concatenate([x for x, _ in blocks], axis=0)
    offsets = [offset for _, offsets in blocks for offset in offsets]
    blocks = [everything, exchange(everything, devices, 1)]
    offsets += [offset ^ 1 for offset in offsets]

    return pl.pallas_call(
        functools.partial(score_kernel, offsets, own_queries),
        out_shape=jax.ShapeDtypeStruct((sequences, queries), f32),
        in_specs=[in_vmem] * (1 + len(blocks)),
        out_specs=in_vmem,
        scratch_shapes=[pltpu.VMEM((sequences, queries * 8, 2 * width), f32)],
        compiler_params=params,
        name="scores",
    )(train, *blocks)


def solution(mesh):
    return jax.shard_map(
        per_device,
        mesh=mesh,
        in_specs=(
            P(("group", "dp"), None),
            P(("group", "dp"), None),
            P(("group", "dp"), None),
            P(("group", "dp"), None),
            P(),
            P(),
            P(),
            P(),
            P(("group", "dp")),
        ),
        out_specs=P(("group", "dp"), None),
        check_vma=False,
    )
```

profile of v0, /device:TPU:0, one launch (start us, length us, event | category | flops | bytes accessed | tf_op | source)
XLA Modules:
  0.0 31.7 jit_solution(16146523354506167318)
XLA Ops:
  0.7 6.7 %front.1 = (f32[72,128]{1,0:T(8,128)S(1)}, f32[4,64,256]{2,1,0:T(8,128)S(1)}, f32[1,96,128]{2,1,0:T(8,128)S(1)}) custom-call(s32[1]{0:T(128)S(6)} %copy.17.ids, bf16[512,4096]{1,0:T(8,128)(2,1)} %acts.1, bf16[512,4096]{1,0:T(8,128)(2,1)} %grad_q.1, bf16[512,1024]{1,0:T(8,128)(2,1)} %grad_k.1, bf16[512,1024]{1,0:T(8,128)(2,1)} %grad_v.1, ...), custom_call_target="tpu_custom_call" | custom-call | tf_op jit(solution)/shard_map/front/pallas_call | solution.py:251
  7.3 0.5 %collective-permute-start = (f32[72,128]{1,0:T(8,128)S(1)}, f32[72,128]{1,0:T(8,128)S(1)}, u32[]{:S(2)}, u32[]{:S(2)}) collective-permute-start(f32[72,128]{1,0:T(8,128)S(1)} %get-tuple-element.17), channel_id=1, source_target_pairs={{0,1},{1,0},{2,3},{3,2},{4,5},{5,4},{6,7},{7,6},{8,9},{9,8},{10,11... | collective-permute-start | bytes 110600 | tf_op jit(solution)/shard_map/ppermute | solution.py:233
  7.9 3.7 %collective-permute-start.4 = (f32[1,96,128]{2,1,0:T(8,128)S(1)}, f32[1,96,128]{2,1,0:T(8,128)S(1)}, u32[]{:S(2)}, u32[]{:S(2)}) collective-permute-start(f32[1,96,128]{2,1,0:T(8,128)S(1)} %get-tuple-element.24), channel_id=1, source_target_pairs={{0,8},{1,9},{2,10},{3,11},{4,12},{5,13},{6,14},{7,15},{8,0},{9,1},... | collective-permute-start | bytes 147464 | tf_op jit(solution)/shard_map/ppermute | solution.py:233
  11.5 0.0 collective-permute-done
  11.5 1.6 %collective-permute-start.1 = (f32[72,128]{1,0:T(8,128)S(1)}, f32[72,128]{1,0:T(8,128)S(1)}, u32[]{:S(2)}, u32[]{:S(2)}) collective-permute-start(f32[72,128]{1,0:T(8,128)S(1)} %add.9), channel_id=1, source_target_pairs={{0,4},{1,5},{2,6},{3,7},{4,0},{5,1},{6,2},{7,3},{8,12},{9,13},{10,... | collective-permute-start | bytes 110600 | tf_op jit(solution)/shard_map/ppermute | solution.py:233
  13.2 1.5 %collective-permute-start.10 = (f32[1,96,128]{2,1,0:T(8,128)S(1)}, f32[1,96,128]{2,1,0:T(8,128)S(1)}, u32[]{:S(2)}, u32[]{:S(2)}) collective-permute-start(f32[1,96,128]{2,1,0:T(8,128)S(1)} %get-tuple-element.24), channel_id=1, source_target_pairs={{0,2},{1,3},{2,0},{3,1},{4,6},{5,7},{6,4},{7,5},{8,10},{9,11},{10,... | collective-permute-start | bytes 147464 | tf_op jit(solution)/shard_map/ppermute | solution.py:233
  14.7 0.9 %collective-permute-done.1 = f32[72,128]{1,0:T(8,128)S(1)} collective-permute-done((f32[72,128]{1,0:T(8,128)S(1)}, f32[72,128]{1,0:T(8,128)S(1)}, u32[]{:S(2)}, u32[]{:S(2)}) %collective-permute-start.1) | collective-permute-done | bytes 36896 | tf_op jit(solution)/shard_map/ppermute | solution.py:233
  15.6 1.5 %collective-permute-start.2 = (f32[72,128]{1,0:T(8,128)S(1)}, f32[72,128]{1,0:T(8,128)S(1)}, u32[]{:S(2)}, u32[]{:S(2)}) collective-permute-start(f32[72,128]{1,0:T(8,128)S(1)} %add.10), channel_id=1, source_target_pairs={{0,2},{1,3},{2,0},{3,1},{4,6},{5,7},{6,4},{7,5},{8,10},{9,11},{10,... | collective-permute-start | bytes 110600 | tf_op jit(solution)/shard_map/ppermute | solution.py:233
  17.1 0.0 collective-permute-done.4
  17.1 1.6 %collective-permute-start.6 = (f32[1,96,128]{2,1,0:T(8,128)S(1)}, f32[1,96,128]{2,1,0:T(8,128)S(1)}, u32[]{:S(2)}, u32[]{:S(2)}) collective-permute-start(f32[1,96,128]{2,1,0:T(8,128)S(1)} %collective-permute-done.4), channel_id=1, source_target_pairs={{0,4},{1,5},{2,6},{3,7},{4,0},{5,1},{6,2},{7,3},{8,12},{9,13},{10,... | collective-permute-start | bytes 147464 | tf_op jit(solution)/shard_map/ppermute | solution.py:233
  18.7 0.5 %collective-permute-start.7 = (f32[1,96,128]{2,1,0:T(8,128)S(1)}, f32[1,96,128]{2,1,0:T(8,128)S(1)}, u32[]{:S(2)}, u32[]{:S(2)}) collective-permute-start(f32[1,96,128]{2,1,0:T(8,128)S(1)} %collective-permute-done.4), channel_id=1, source_target_pairs={{0,2},{1,3},{2,0},{3,1},{4,6},{5,7},{6,4},{7,5},{8,10},{9,11},{10,... | collective-permute-start | bytes 147464 | tf_op jit(solution)/shard_map/ppermute | solution.py:233
  19.2 0.4 %collective-permute-start.5 = (f32[1,96,128]{2,1,0:T(8,128)S(1)}, f32[1,96,128]{2,1,0:T(8,128)S(1)}, u32[]{:S(2)}, u32[]{:S(2)}) collective-permute-start(f32[1,96,128]{2,1,0:T(8,128)S(1)} %get-tuple-element.24), channel_id=1, source_target_pairs={{0,4},{1,5},{2,6},{3,7},{4,0},{5,1},{6,2},{7,3},{8,12},{9,13},{10,... | collective-permute-start | bytes 147464 | tf_op jit(solution)/shard_map/ppermute | solution.py:233
  19.6 0.0 collective-permute-done.2
  19.6 1.7 %collective-permute-start.3 = (f32[72,128]{1,0:T(8,128)S(1)}, f32[72,128]{1,0:T(8,128)S(1)}, u32[]{:S(2)}, u32[]{:S(2)}) collective-permute-start(f32[72,128]{1,0:T(8,128)S(1)} %add.11.first), channel_id=1, source_target_pairs={{0,8},{1,9},{2,10},{3,11},{4,12},{5,13},{6,14},{7,15},{8,0},{9,1},... | collective-permute-start | bytes 110600 | tf_op jit(solution)/shard_map/ppermute | solution.py:233
  21.3 1.9 %collective-permute-done.5 = f32[1,96,128]{2,1,0:T(8,128)S(1)} collective-permute-done((f32[1,96,128]{2,1,0:T(8,128)S(1)}, f32[1,96,128]{2,1,0:T(8,128)S(1)}, u32[]{:S(2)}, u32[]{:S(2)}) %collective-permute-start.5) | collective-permute-done | bytes 49184 | tf_op jit(solution)/shard_map/ppermute | solution.py:233
  23.3 0.0 collective-permute-done.6
  23.3 1.5 %collective-permute-start.8 = (f32[1,96,128]{2,1,0:T(8,128)S(1)}, f32[1,96,128]{2,1,0:T(8,128)S(1)}, u32[]{:S(2)}, u32[]{:S(2)}) collective-permute-start(f32[1,96,128]{2,1,0:T(8,128)S(1)} %collective-permute-done.5), channel_id=1, source_target_pairs={{0,2},{1,3},{2,0},{3,1},{4,6},{5,7},{6,4},{7,5},{8,10},{9,11},{10,... | collective-permute-start | bytes 147464 | tf_op jit(solution)/shard_map/ppermute | solution.py:233
  24.8 0.5 %collective-permute-start.9 = (f32[1,96,128]{2,1,0:T(8,128)S(1)}, f32[1,96,128]{2,1,0:T(8,128)S(1)}, u32[]{:S(2)}, u32[]{:S(2)}) collective-permute-start(f32[1,96,128]{2,1,0:T(8,128)S(1)} %collective-permute-done.6), channel_id=1, source_target_pairs={{0,2},{1,3},{2,0},{3,1},{4,6},{5,7},{6,4},{7,5},{8,10},{9,11},{10,... | collective-permute-start | bytes 147464 | tf_op jit(solution)/shard_map/ppermute | solution.py:233
  25.3 0.0 collective-permute-done.3.second
  25.3 2.5 %invert.1.train = f32[4,96,128]{2,1,0:T(8,128)S(1)} custom-call(f32[72,128]{1,0:T(8,128)S(1)} %add.11.first, f32[72,128]{1,0:T(8,128)S(1)} %collective-permute-done.3.second, f32[4,64,256]{2,1,0:T(8,128)S(1)} %get-tuple-element.18.grams), custom_call_target="tpu_custom_call" | custom-call | tf_op jit(solution)/shard_map/invert/pallas_call | solution.py:301
  27.8 0.0 collective-permute-done.10
  27.9 0.0 collective-permute-done.7
  27.9 0.0 collective-permute-done.8
  27.9 1.0 %collective-permute-done.9 = f32[1,96,128]{2,1,0:T(8,128)S(1)} collective-permute-done((f32[1,96,128]{2,1,0:T(8,128)S(1)}, f32[1,96,128]{2,1,0:T(8,128)S(1)}, u32[]{:S(2)}, u32[]{:S(2)}) %collective-permute-start.9) | collective-permute-done | bytes 49184 | tf_op jit(solution)/shard_map/ppermute | solution.py:233
  28.9 0.1 collective-permute-start.11
  29.0 1.7 %collective-permute-done.11.refs_1_ = f32[8,96,128]{2,1,0:T(8,128)S(1)} collective-permute-done((f32[8,96,128]{2,1,0:T(8,128)S(1)}, f32[8,96,128]{2,1,0:T(8,128)S(1)}, u32[]{:S(2)}, u32[]{:S(2)}) %collective-permute-start.11) | collective-permute-done | bytes 393248 | tf_op jit(solution)/shard_map/ppermute | solution.py:233
  30.7 1.0 %scores.1 = f32[4,16]{1,0:T(4,128)} custom-call(f32[4,96,128]{2,1,0:T(8,128)S(1)} %invert.1.train, f32[8,96,128]{2,1,0:T(8,128)S(1)} %constant_dynamic-update-slice_fusion.refs_0_, f32[8,96,128]{2,1,0:T(8,128)S(1)} %collective-permute-done.11.refs_1_), custom_call_target="tpu_custom_call" | custom-call | tf_op jit(solution)/shard_map/scores/pallas_call | solution.py:319
  (11 shorter events, 0.1 us)
Async XLA Ops:
  7.3 4.2 %collective-permute-start = (f32[72,128]{1,0:T(8,128)S(1)}, f32[72,128]{1,0:T(8,128)S(1)}, u32[]{:S(2)}, u32[]{:S(2)}) collective-permute-start(f32[72,128]{1,0:T(8,128)S(1)} %get-tuple-element.17), channel_id=1, source_target_pairs={{0,1},{1,0},{2,3},{3,2},{4,5},{5,4},{6,7},{7,6},{8,9},{9,8},{10,11... | collective-permute-start | bytes 110600 | tf_op jit(solution)/shard_map/ppermute | solution.py:233
  7.9 9.2 %collective-permute-start.4 = (f32[1,96,128]{2,1,0:T(8,128)S(1)}, f32[1,96,128]{2,1,0:T(8,128)S(1)}, u32[]{:S(2)}, u32[]{:S(2)}) collective-permute-start(f32[1,96,128]{2,1,0:T(8,128)S(1)} %get-tuple-element.24), channel_id=1, source_target_pairs={{0,8},{1,9},{2,10},{3,11},{4,12},{5,13},{6,14},{7,15},{8,0},{9,1},... | collective-permute-start | bytes 147464 | tf_op jit(solution)/shard_map/ppermute | solution.py:233
  11.5 4.0 %collective-permute-start.1 = (f32[72,128]{1,0:T(8,128)S(1)}, f32[72,128]{1,0:T(8,128)S(1)}, u32[]{:S(2)}, u32[]{:S(2)}) collective-permute-start(f32[72,128]{1,0:T(8,128)S(1)} %add.9), channel_id=1, source_target_pairs={{0,4},{1,5},{2,6},{3,7},{4,0},{5,1},{6,2},{7,3},{8,12},{9,13},{10,... | collective-permute-start | bytes 110600 | tf_op jit(solution)/shard_map/ppermute | solution.py:233
  13.2 14.7 %collective-permute-start.10 = (f32[1,96,128]{2,1,0:T(8,128)S(1)}, f32[1,96,128]{2,1,0:T(8,128)S(1)}, u32[]{:S(2)}, u32[]{:S(2)}) collective-permute-start(f32[1,96,128]{2,1,0:T(8,128)S(1)} %get-tuple-element.24), channel_id=1, source_target_pairs={{0,2},{1,3},{2,0},{3,1},{4,6},{5,7},{6,4},{7,5},{8,10},{9,11},{10,... | collective-permute-start | bytes 147464 | tf_op jit(solution)/shard_map/ppermute | solution.py:233
  15.6 4.1 %collective-permute-start.2 = (f32[72,128]{1,0:T(8,128)S(1)}, f32[72,128]{1,0:T(8,128)S(1)}, u32[]{:S(2)}, u32[]{:S(2)}) collective-permute-start(f32[72,128]{1,0:T(8,128)S(1)} %add.10), channel_id=1, source_target_pairs={{0,2},{1,3},{2,0},{3,1},{4,6},{5,7},{6,4},{7,5},{8,10},{9,11},{10,... | collective-permute-start | bytes 110600 | tf_op jit(solution)/shard_map/ppermute | solution.py:233
  17.1 6.2 %collective-permute-start.6 = (f32[1,96,128]{2,1,0:T(8,128)S(1)}, f32[1,96,128]{2,1,0:T(8,128)S(1)}, u32[]{:S(2)}, u32[]{:S(2)}) collective-permute-start(f32[1,96,128]{2,1,0:T(8,128)S(1)} %collective-permute-done.4), channel_id=1, source_target_pairs={{0,4},{1,5},{2,6},{3,7},{4,0},{5,1},{6,2},{7,3},{8,12},{9,13},{10,... | collective-permute-start | bytes 147464 | tf_op jit(solution)/shard_map/ppermute | solution.py:233
  18.7 9.2 %collective-permute-start.7 = (f32[1,96,128]{2,1,0:T(8,128)S(1)}, f32[1,96,128]{2,1,0:T(8,128)S(1)}, u32[]{:S(2)}, u32[]{:S(2)}) collective-permute-start(f32[1,96,128]{2,1,0:T(8,128)S(1)} %collective-permute-done.4), channel_id=1, source_target_pairs={{0,2},{1,3},{2,0},{3,1},{4,6},{5,7},{6,4},{7,5},{8,10},{9,11},{10,... | collective-permute-start | bytes 147464 | tf_op jit(solution)/shard_map/ppermute | solution.py:233
  19.2 4.1 %collective-permute-start.5 = (f32[1,96,128]{2,1,0:T(8,128)S(1)}, f32[1,96,128]{2,1,0:T(8,128)S(1)}, u32[]{:S(2)}, u32[]{:S(2)}) collective-permute-start(f32[1,96,128]{2,1,0:T(8,128)S(1)} %get-tuple-element.24), channel_id=1, source_target_pairs={{0,4},{1,5},{2,6},{3,7},{4,0},{5,1},{6,2},{7,3},{8,12},{9,13},{10,... | collective-permute-start | bytes 147464 | tf_op jit(solution)/shard_map/ppermute | solution.py:233
  19.6 5.7 %collective-permute-start.3 = (f32[72,128]{1,0:T(8,128)S(1)}, f32[72,128]{1,0:T(8,128)S(1)}, u32[]{:S(2)}, u32[]{:S(2)}) collective-permute-start(f32[72,128]{1,0:T(8,128)S(1)} %add.11.first), channel_id=1, source_target_pairs={{0,8},{1,9},{2,10},{3,11},{4,12},{5,13},{6,14},{7,15},{8,0},{9,1},... | collective-permute-start | bytes 110600 | tf_op jit(solution)/shard_map/ppermute | solution.py:233
  23.3 4.6 %collective-permute-start.8 = (f32[1,96,128]{2,1,0:T(8,128)S(1)}, f32[1,96,128]{2,1,0:T(8,128)S(1)}, u32[]{:S(2)}, u32[]{:S(2)}) collective-permute-start(f32[1,96,128]{2,1,0:T(8,128)S(1)} %collective-permute-done.5), channel_id=1, source_target_pairs={{0,2},{1,3},{2,0},{3,1},{4,6},{5,7},{6,4},{7,5},{8,10},{9,11},{10,... | collective-permute-start | bytes 147464 | tf_op jit(solution)/shard_map/ppermute | solution.py:233
  24.8 4.1 %collective-permute-start.9 = (f32[1,96,128]{2,1,0:T(8,128)S(1)}, f32[1,96,128]{2,1,0:T(8,128)S(1)}, u32[]{:S(2)}, u32[]{:S(2)}) collective-permute-start(f32[1,96,128]{2,1,0:T(8,128)S(1)} %collective-permute-done.6), channel_id=1, source_target_pairs={{0,2},{1,3},{2,0},{3,1},{4,6},{5,7},{6,4},{7,5},{8,10},{9,11},{10,... | collective-permute-start | bytes 147464 | tf_op jit(solution)/shard_map/ppermute | solution.py:233
  28.9 1.8 %collective-permute-start.11 = (f32[8,96,128]{2,1,0:T(8,128)S(1)}, f32[8,96,128]{2,1,0:T(8,128)S(1)}, u32[]{:S(2)}, u32[]{:S(2)}) collective-permute-start(f32[8,96,128]{2,1,0:T(8,128)S(1)} %constant_dynamic-update-slice_fusion.refs_0_), channel_id=1, source_target_pairs={{0,1},{1,0},{2,3},{3,2},{4,5},{5,4},{6,7},{7,6},{8,9},{9,8},{10,11... | collective-permute-start | bytes 1179656 | tf_op jit(solution)/shard_map/ppermute | solution.py:233
where the time goes:
time: 31.9 us; the launch traced here: 31.7 us
  starting transfers between devices  15.2 us (48%)
  Pallas kernels  10.2 us (32%)
  waiting for transfers between devices  5.52 us (17%)
  between operations  0.75 us (2%)
    ppermute x12, starting transfers between devices, exchange(): return lax.ppermute(x, 'dp', [(i, i ^ distance) for i in range(devices)])  15.2 us
    pallas_call x1, Pallas kernels, per_device(): pl.pallas_call(functools.partial(front_kernel, tokens * devices, sequence...  6.67 us
    ppermute x12, waiting for transfers between devices, exchange(): return lax.ppermute(x, 'dp', [(i, i ^ distance) for i in range(devices)])  5.52 us
    pallas_call x1, Pallas kernels, per_device(): pl.pallas_call(functools.partial(invert_kernel, sequences, width), out_sh...  2.54 us
    pallas_call x1, Pallas kernels, per_device(): pl.pallas_call(functools.partial(score_kernel, offsets, own_queries), out...  1.02 us
  transfers between devices with their start and end apart: 12, of which 4 were waited for; matrix products, arithmetic and copies ran while one was open for 0% of the time, Pallas kernels for 8%

commit v1 on v0

--- a/solution.py
+++ b/solution.py
@@ -263,9 +263,6 @@
         name="front",
     )(query_ids, *tables)
 
-    factor_bits = list(range(steps))
-    if steps > 2:
-        factor_bits[1], factor_bits[2] = 2, 1
     query_bits = list(range(1, steps))[::-1]
 
     def send(items, bit):
@@ -283,10 +280,15 @@
         arrays = lax.optimization_barrier((*[x for x, _ in items], token))[:-1]
         return [(x, offsets) for x, (_, offsets) in zip(arrays, items)]
 
+    def both_cores(items):
+        joined = jnp.concatenate([x for x, _ in items], axis=0)
+        offsets = [offset for _, part in items for offset in part]
+        return [(joined, offsets), (exchange(joined, devices, 1), [offset ^ 1 for offset in offsets])]
+
     own = [(query, [0])]
     mine, blocks, pending, early = factors, [], [], []
     for step in range(steps):
-        theirs = exchange(mine, devices, 1 << factor_bits[step])
+        theirs = exchange(mine, devices, 1 << step)
         if step == 0:
             pending = send(own, query_bits[0])
         elif step == 1:
@@ -295,6 +297,8 @@
             blocks += after(pending, mine)
             last = step == steps - 1
             pending = send(([] if last else after(own, mine)) + blocks, query_bits[step - 1])
+            if last:
+                first = both_cores(own + blocks)
         if step < steps - 1:
             mine = mine + theirs
     terms = (mine, theirs)
@@ -310,11 +314,9 @@
         compiler_params=params,
         name="invert",
     )(*terms, grams)
-    blocks = own + blocks + after(pending + early, train)
-    everything = jnp.concatenate([x for x, _ in blocks], axis=0)
-    offsets = [offset for _, offsets in blocks for offset in offsets]
-    blocks = [everything, exchange(everything, devices, 1)]
-    offsets += [offset ^ 1 for offset in offsets]
+    last = both_cores(after(pending + early, train))
+    blocks = [x for x, _ in first + last]
+    offsets = [offset for _, offsets in first + last for offset in offsets]
 
     return pl.pallas_call(
         functools.partial(score_kernel, offsets, own_queries),

time: 31.9 us -> 31.5 us (0.987)
  waiting for transfers between devices: 5.52 us -> 5.05 us
    ppermute x12 -> x13, waiting for transfers between devices: 5.52 us -> 5.05 us  [exchange(): return lax.ppermute(x, 'dp', [(i, i ^ distance) for i in range(devices)])]
    ppermute x12 -> x13, starting transfers between devices: 15.2 us -> 15.2 us  [exchange(): return lax.ppermute(x, 'dp', [(i, i ^ distance) for i in range(devices)])]
  transfers between devices with their start and end apart: 12 -> 13, of which waited for: 4 -> 4; matrix products, arithmetic and copies ran while one was open for 0% -> 0% of each run, Pallas kernels for 8% -> 8%
where the time goes in v1:
time: 31.5 us; the launch traced here: 31.3 us
  starting transfers between devices  15.2 us (48%)
  Pallas kernels  10.2 us (32%)
  waiting for transfers between devices  5.05 us (16%)
  between operations  0.76 us (2%)
    ppermute x13, starting transfers between devices, exchange(): return lax.ppermute(x, 'dp', [(i, i ^ distance) for i in range(devices)])  15.2 us
    pallas_call x1, Pallas kernels, per_device(): pl.pallas_call(functools.partial(front_kernel, tokens * devices, sequence...  6.67 us
    ppermute x13, waiting for transfers between devices, exchange(): return lax.ppermute(x, 'dp', [(i, i ^ distance) for i in range(devices)])  5.05 us
    pallas_call x1, Pallas kernels, per_device(): pl.pallas_call(functools.partial(invert_kernel, sequences, width), out_sh...  2.53 us
    pallas_call x1, Pallas kernels, per_device(): pl.pallas_call(functools.partial(score_kernel, offsets, own_queries), out...  1.02 us
  transfers between devices with their start and end apart: 13, of which 4 were waited for; matrix products, arithmetic and copies ran while one was open for 0% of the time, Pallas kernels for 8%

profile of v1, /device:TPU:0, one launch (start us, length us, event | category | flops | bytes accessed | tf_op | source)
XLA Modules:
  0.0 31.3 jit_solution(11657423774001730460)
XLA Ops:
  0.7 6.7 %front.1 = (f32[72,128]{1,0:T(8,128)S(1)}, f32[4,64,256]{2,1,0:T(8,128)S(1)}, f32[1,96,128]{2,1,0:T(8,128)S(1)}) custom-call(s32[1]{0:T(128)S(6)} %copy.16.ids, bf16[512,4096]{1,0:T(8,128)(2,1)} %acts.1, bf16[512,4096]{1,0:T(8,128)(2,1)} %grad_q.1, bf16[512,1024]{1,0:T(8,128)(2,1)} %grad_k.1, bf16[512,1024]{1,0:T(8,128)(2,1)} %grad_v.1, ...), custom_call_target="tpu_custom_call" | custom-call | tf_op jit(solution)/shard_map/front/pallas_call | solution.py:251
  7.3 0.5 %collective-permute-start = (f32[72,128]{1,0:T(8,128)S(1)}, f32[72,128]{1,0:T(8,128)S(1)}, u32[]{:S(2)}, u32[]{:S(2)}) collective-permute-start(f32[72,128]{1,0:T(8,128)S(1)} %get-tuple-element.17), channel_id=1, source_target_pairs={{0,1},{1,0},{2,3},{3,2},{4,5},{5,4},{6,7},{7,6},{8,9},{9,8},{10,11... | collective-permute-start | bytes 110600 | tf_op jit(solution)/shard_map/ppermute | solution.py:233
  7.9 3.7 %collective-permute-start.4 = (f32[1,96,128]{2,1,0:T(8,128)S(1)}, f32[1,96,128]{2,1,0:T(8,128)S(1)}, u32[]{:S(2)}, u32[]{:S(2)}) collective-permute-start(f32[1,96,128]{2,1,0:T(8,128)S(1)} %get-tuple-element.24), channel_id=1, source_target_pairs={{0,8},{1,9},{2,10},{3,11},{4,12},{5,13},{6,14},{7,15},{8,0},{9,1},... | collective-permute-start | bytes 147464 | tf_op jit(solution)/shard_map/ppermute | solution.py:233
  11.5 0.0 collective-permute-done
  11.5 1.6 %collective-permute-start.1 = (f32[72,128]{1,0:T(8,128)S(1)}, f32[72,128]{1,0:T(8,128)S(1)}, u32[]{:S(2)}, u32[]{:S(2)}) collective-permute-start(f32[72,128]{1,0:T(8,128)S(1)} %add.9), channel_id=1, source_target_pairs={{0,2},{1,3},{2,0},{3,1},{4,6},{5,7},{6,4},{7,5},{8,10},{9,11},{10,... | collective-permute-start | bytes 110600 | tf_op jit(solution)/shard_map/ppermute | solution.py:233
  13.1 0.5 %collective-permute-start.11 = (f32[1,96,128]{2,1,0:T(8,128)S(1)}, f32[1,96,128]{2,1,0:T(8,128)S(1)}, u32[]{:S(2)}, u32[]{:S(2)}) collective-permute-start(f32[1,96,128]{2,1,0:T(8,128)S(1)} %get-tuple-element.24), channel_id=1, source_target_pairs={{0,2},{1,3},{2,0},{3,1},{4,6},{5,7},{6,4},{7,5},{8,10},{9,11},{10,... | collective-permute-start | bytes 147464 | tf_op jit(solution)/shard_map/ppermute | solution.py:233
  13.6 1.9 %collective-permute-done.1 = f32[72,128]{1,0:T(8,128)S(1)} collective-permute-done((f32[72,128]{1,0:T(8,128)S(1)}, f32[72,128]{1,0:T(8,128)S(1)}, u32[]{:S(2)}, u32[]{:S(2)}) %collective-permute-start.1) | collective-permute-done | bytes 36896 | tf_op jit(solution)/shard_map/ppermute | solution.py:233
  15.6 1.6 %collective-permute-start.2 = (f32[72,128]{1,0:T(8,128)S(1)}, f32[72,128]{1,0:T(8,128)S(1)}, u32[]{:S(2)}, u32[]{:S(2)}) collective-permute-start(f32[72,128]{1,0:T(8,128)S(1)} %add.10), channel_id=1, source_target_pairs={{0,4},{1,5},{2,6},{3,7},{4,0},{5,1},{6,2},{7,3},{8,12},{9,13},{10,... | collective-permute-start | bytes 110600 | tf_op jit(solution)/shard_map/ppermute | solution.py:233
  17.1 0.0 collective-permute-done.4
  17.1 1.6 %collective-permute-start.8 = (f32[1,96,128]{2,1,0:T(8,128)S(1)}, f32[1,96,128]{2,1,0:T(8,128)S(1)}, u32[]{:S(2)}, u32[]{:S(2)}) collective-permute-start(f32[1,96,128]{2,1,0:T(8,128)S(1)} %collective-permute-done.4), channel_id=1, source_target_pairs={{0,2},{1,3},{2,0},{3,1},{4,6},{5,7},{6,4},{7,5},{8,10},{9,11},{10,... | collective-permute-start | bytes 147464 | tf_op jit(solution)/shard_map/ppermute | solution.py:233
  18.8 0.4 %collective-permute-start.6 = (f32[1,96,128]{2,1,0:T(8,128)S(1)}, f32[1,96,128]{2,1,0:T(8,128)S(1)}, u32[]{:S(2)}, u32[]{:S(2)}) collective-permute-start(f32[1,96,128]{2,1,0:T(8,128)S(1)} %collective-permute-done.4), channel_id=1, source_target_pairs={{0,4},{1,5},{2,6},{3,7},{4,0},{5,1},{6,2},{7,3},{8,12},{9,13},{10,... | collective-permute-start | bytes 147464 | tf_op jit(solution)/shard_map/ppermute | solution.py:233
  19.2 1.6 %collective-permute-start.5 = (f32[1,96,128]{2,1,0:T(8,128)S(1)}, f32[1,96,128]{2,1,0:T(8,128)S(1)}, u32[]{:S(2)}, u32[]{:S(2)}) collective-permute-start(f32[1,96,128]{2,1,0:T(8,128)S(1)} %get-tuple-element.24), channel_id=1, source_target_pairs={{0,4},{1,5},{2,6},{3,7},{4,0},{5,1},{6,2},{7,3},{8,12},{9,13},{10,... | collective-permute-start | bytes 147464 | tf_op jit(solution)/shard_map/ppermute | solution.py:233
  20.8 0.0 collective-permute-done.2
  20.8 1.1 %collective-permute-start.3 = (f32[72,128]{1,0:T(8,128)S(1)}, f32[72,128]{1,0:T(8,128)S(1)}, u32[]{:S(2)}, u32[]{:S(2)}) collective-permute-start(f32[72,128]{1,0:T(8,128)S(1)} %add.11.first), channel_id=1, source_target_pairs={{0,8},{1,9},{2,10},{3,11},{4,12},{5,13},{6,14},{7,15},{8,0},{9,1},... | collective-permute-start | bytes 110600 | tf_op jit(solution)/shard_map/ppermute | solution.py:233
  21.9 1.7 %collective-permute-done.5 = f32[1,96,128]{2,1,0:T(8,128)S(1)} collective-permute-done((f32[1,96,128]{2,1,0:T(8,128)S(1)}, f32[1,96,128]{2,1,0:T(8,128)S(1)}, u32[]{:S(2)}, u32[]{:S(2)}) %collective-permute-start.5) | collective-permute-done | bytes 49184 | tf_op jit(solution)/shard_map/ppermute | solution.py:233
  23.6 0.0 collective-permute-done.6
  23.6 0.5 %collective-permute-start.9 = (f32[1,96,128]{2,1,0:T(8,128)S(1)}, f32[1,96,128]{2,1,0:T(8,128)S(1)}, u32[]{:S(2)}, u32[]{:S(2)}) collective-permute-start(f32[1,96,128]{2,1,0:T(8,128)S(1)} %collective-permute-done.5), channel_id=1, source_target_pairs={{0,2},{1,3},{2,0},{3,1},{4,6},{5,7},{6,4},{7,5},{8,10},{9,11},{10,... | collective-permute-start | bytes 147464 | tf_op jit(solution)/shard_map/ppermute | solution.py:233
  24.1 1.5 %collective-permute-start.10 = (f32[1,96,128]{2,1,0:T(8,128)S(1)}, f32[1,96,128]{2,1,0:T(8,128)S(1)}, u32[]{:S(2)}, u32[]{:S(2)}) collective-permute-start(f32[1,96,128]{2,1,0:T(8,128)S(1)} %collective-permute-done.6), channel_id=1, source_target_pairs={{0,2},{1,3},{2,0},{3,1},{4,6},{5,7},{6,4},{7,5},{8,10},{9,11},{10,... | collective-permute-start | bytes 147464 | tf_op jit(solution)/shard_map/ppermute | solution.py:233
  25.7 0.4 %collective-permute-done.3.second = f32[72,128]{1,0:T(8,128)S(1)} collective-permute-done((f32[72,128]{1,0:T(8,128)S(1)}, f32[72,128]{1,0:T(8,128)S(1)}, u32[]{:S(2)}, u32[]{:S(2)}) %collective-permute-start.3) | collective-permute-done | bytes 36896 | tf_op jit(solution)/shard_map/ppermute | solution.py:233
  26.0 0.0 collective-permute-start.7
  26.0 2.5 %invert.1.train = f32[4,96,128]{2,1,0:T(8,128)S(1)} custom-call(f32[72,128]{1,0:T(8,128)S(1)} %add.11.first, f32[72,128]{1,0:T(8,128)S(1)} %collective-permute-done.3.second, f32[4,64,256]{2,1,0:T(8,128)S(1)} %get-tuple-element.18.grams), custom_call_target="tpu_custom_call" | custom-call | tf_op jit(solution)/shard_map/invert/pallas_call | solution.py:305
  28.6 0.0 collective-permute-done.11
  28.6 0.0 collective-permute-done.8
  28.6 0.0 collective-permute-done.9
  28.6 0.0 collective-permute-done.10
  28.7 0.6 %collective-permute-start.12 = (f32[4,96,128]{2,1,0:T(8,128)S(1)}, f32[4,96,128]{2,1,0:T(8,128)S(1)}, u32[]{:S(2)}, u32[]{:S(2)}) collective-permute-start(f32[4,96,128]{2,1,0:T(8,128)S(1)} %constant_dynamic-update-slice_fusion.4.refs_2_), channel_id=1, source_target_pairs={{0,1},{1,0},{2,3},{3,2},{4,5},{5,4},{6,7},{7,6},{8,9},{9,8},{10,11... | collective-permute-start | bytes 589832 | tf_op jit(solution)/shard_map/ppermute | solution.py:233
  29.2 0.0 collective-permute-done.7.refs_1_
  29.2 1.1 %collective-permute-done.12.refs_3_ = f32[4,96,128]{2,1,0:T(8,128)S(1)} collective-permute-done((f32[4,96,128]{2,1,0:T(8,128)S(1)}, f32[4,96,128]{2,1,0:T(8,128)S(1)}, u32[]{:S(2)}, u32[]{:S(2)}) %collective-permute-start.12) | collective-permute-done | bytes 196640 | tf_op jit(solution)/shard_map/ppermute | solution.py:233
  30.3 1.0 %scores.1 = f32[4,16]{1,0:T(4,128)} custom-call(f32[4,96,128]{2,1,0:T(8,128)S(1)} %invert.1.train, f32[4,96,128]{2,1,0:T(8,128)S(1)} %constant_dynamic-update-slice_fusion.refs_0_, f32[4,96,128]{2,1,0:T(8,128)S(1)} %collective-permute-done.7.refs_1_, f32[4,96,128]{2,1,0:T(8,128)S(1)} %constant_dynamic-update-slice_fusion.4.refs_2_, ...), custom_call_target="tpu_custom_call" | custom-call | tf_op jit(solution)/shard_map/scores/pallas_call | solution.py:321
  (11 shorter events, 0.1 us)
Async XLA Ops:
  7.3 4.2 %collective-permute-start = (f32[72,128]{1,0:T(8,128)S(1)}, f32[72,128]{1,0:T(8,128)S(1)}, u32[]{:S(2)}, u32[]{:S(2)}) collective-permute-start(f32[72,128]{1,0:T(8,128)S(1)} %get-tuple-element.17), channel_id=1, source_target_pairs={{0,1},{1,0},{2,3},{3,2},{4,5},{5,4},{6,7},{7,6},{8,9},{9,8},{10,11... | collective-permute-start | bytes 110600 | tf_op jit(solution)/shard_map/ppermute | solution.py:233
  7.9 9.3 %collective-permute-start.4 = (f32[1,96,128]{2,1,0:T(8,128)S(1)}, f32[1,96,128]{2,1,0:T(8,128)S(1)}, u32[]{:S(2)}, u32[]{:S(2)}) collective-permute-start(f32[1,96,128]{2,1,0:T(8,128)S(1)} %get-tuple-element.24), channel_id=1, source_target_pairs={{0,8},{1,9},{2,10},{3,11},{4,12},{5,13},{6,14},{7,15},{8,0},{9,1},... | collective-permute-start | bytes 147464 | tf_op jit(solution)/shard_map/ppermute | solution.py:233
  11.5 4.0 %collective-permute-start.1 = (f32[72,128]{1,0:T(8,128)S(1)}, f32[72,128]{1,0:T(8,128)S(1)}, u32[]{:S(2)}, u32[]{:S(2)}) collective-permute-start(f32[72,128]{1,0:T(8,128)S(1)} %add.9), channel_id=1, source_target_pairs={{0,2},{1,3},{2,0},{3,1},{4,6},{5,7},{6,4},{7,5},{8,10},{9,11},{10,... | collective-permute-start | bytes 110600 | tf_op jit(solution)/shard_map/ppermute | solution.py:233
  13.1 15.5 %collective-permute-start.11 = (f32[1,96,128]{2,1,0:T(8,128)S(1)}, f32[1,96,128]{2,1,0:T(8,128)S(1)}, u32[]{:S(2)}, u32[]{:S(2)}) collective-permute-start(f32[1,96,128]{2,1,0:T(8,128)S(1)} %get-tuple-element.24), channel_id=1, source_target_pairs={{0,2},{1,3},{2,0},{3,1},{4,6},{5,7},{6,4},{7,5},{8,10},{9,11},{10,... | collective-permute-start | bytes 147464 | tf_op jit(solution)/shard_map/ppermute | solution.py:233
  15.6 5.3 %collective-permute-start.2 = (f32[72,128]{1,0:T(8,128)S(1)}, f32[72,128]{1,0:T(8,128)S(1)}, u32[]{:S(2)}, u32[]{:S(2)}) collective-permute-start(f32[72,128]{1,0:T(8,128)S(1)} %add.10), channel_id=1, source_target_pairs={{0,4},{1,5},{2,6},{3,7},{4,0},{5,1},{6,2},{7,3},{8,12},{9,13},{10,... | collective-permute-start | bytes 110600 | tf_op jit(solution)/shard_map/ppermute | solution.py:233
  17.1 11.5 %collective-permute-start.8 = (f32[1,96,128]{2,1,0:T(8,128)S(1)}, f32[1,96,128]{2,1,0:T(8,128)S(1)}, u32[]{:S(2)}, u32[]{:S(2)}) collective-permute-start(f32[1,96,128]{2,1,0:T(8,128)S(1)} %collective-permute-done.4), channel_id=1, source_target_pairs={{0,2},{1,3},{2,0},{3,1},{4,6},{5,7},{6,4},{7,5},{8,10},{9,11},{10,... | collective-permute-start | bytes 147464 | tf_op jit(solution)/shard_map/ppermute | solution.py:233
  18.8 4.8 %collective-permute-start.6 = (f32[1,96,128]{2,1,0:T(8,128)S(1)}, f32[1,96,128]{2,1,0:T(8,128)S(1)}, u32[]{:S(2)}, u32[]{:S(2)}) collective-permute-start(f32[1,96,128]{2,1,0:T(8,128)S(1)} %collective-permute-done.4), channel_id=1, source_target_pairs={{0,4},{1,5},{2,6},{3,7},{4,0},{5,1},{6,2},{7,3},{8,12},{9,13},{10,... | collective-permute-start | bytes 147464 | tf_op jit(solution)/shard_map/ppermute | solution.py:233
  19.2 4.4 %collective-permute-start.5 = (f32[1,96,128]{2,1,0:T(8,128)S(1)}, f32[1,96,128]{2,1,0:T(8,128)S(1)}, u32[]{:S(2)}, u32[]{:S(2)}) collective-permute-start(f32[1,96,128]{2,1,0:T(8,128)S(1)} %get-tuple-element.24), channel_id=1, source_target_pairs={{0,4},{1,5},{2,6},{3,7},{4,0},{5,1},{6,2},{7,3},{8,12},{9,13},{10,... | collective-permute-start | bytes 147464 | tf_op jit(solution)/shard_map/ppermute | solution.py:233
  20.8 5.2 %collective-permute-start.3 = (f32[72,128]{1,0:T(8,128)S(1)}, f32[72,128]{1,0:T(8,128)S(1)}, u32[]{:S(2)}, u32[]{:S(2)}) collective-permute-start(f32[72,128]{1,0:T(8,128)S(1)} %add.11.first), channel_id=1, source_target_pairs={{0,8},{1,9},{2,10},{3,11},{4,12},{5,13},{6,14},{7,15},{8,0},{9,1},... | collective-permute-start | bytes 110600 | tf_op jit(solution)/shard_map/ppermute | solution.py:233
  23.6 5.0 %collective-permute-start.9 = (f32[1,96,128]{2,1,0:T(8,128)S(1)}, f32[1,96,128]{2,1,0:T(8,128)S(1)}, u32[]{:S(2)}, u32[]{:S(2)}) collective-permute-start(f32[1,96,128]{2,1,0:T(8,128)S(1)} %collective-permute-done.5), channel_id=1, source_target_pairs={{0,2},{1,3},{2,0},{3,1},{4,6},{5,7},{6,4},{7,5},{8,10},{9,11},{10,... | collective-permute-start | bytes 147464 | tf_op jit(solution)/shard_map/ppermute | solution.py:233
  24.1 4.5 %collective-permute-start.10 = (f32[1,96,128]{2,1,0:T(8,128)S(1)}, f32[1,96,128]{2,1,0:T(8,128)S(1)}, u32[]{:S(2)}, u32[]{:S(2)}) collective-permute-start(f32[1,96,128]{2,1,0:T(8,128)S(1)} %collective-permute-done.6), channel_id=1, source_target_pairs={{0,2},{1,3},{2,0},{3,1},{4,6},{5,7},{6,4},{7,5},{8,10},{9,11},{10,... | collective-permute-start | bytes 147464 | tf_op jit(solution)/shard_map/ppermute | solution.py:233
  26.0 3.2 %collective-permute-start.7 = (f32[4,96,128]{2,1,0:T(8,128)S(1)}, f32[4,96,128]{2,1,0:T(8,128)S(1)}, u32[]{:S(2)}, u32[]{:S(2)}) collective-permute-start(f32[4,96,128]{2,1,0:T(8,128)S(1)} %constant_dynamic-update-slice_fusion.refs_0_), channel_id=1, source_target_pairs={{0,1},{1,0},{2,3},{3,2},{4,5},{5,4},{6,7},{7,6},{8,9},{9,8},{10,11... | collective-permute-start | bytes 589832 | tf_op jit(solution)/shard_map/ppermute | solution.py:233
  28.7 1.6 %collective-permute-start.12 = (f32[4,96,128]{2,1,0:T(8,128)S(1)}, f32[4,96,128]{2,1,0:T(8,128)S(1)}, u32[]{:S(2)}, u32[]{:S(2)}) collective-permute-start(f32[4,96,128]{2,1,0:T(8,128)S(1)} %constant_dynamic-update-slice_fusion.4.refs_2_), channel_id=1, source_target_pairs={{0,1},{1,0},{2,3},{3,2},{4,5},{5,4},{6,7},{7,6},{8,9},{9,8},{10,11... | collective-permute-start | bytes 589832 | tf_op jit(solution)/shard_map/ppermute | solution.py:233

commit v2 on v1

--- a/solution.py
+++ b/solution.py
@@ -223,10 +223,12 @@
                 product = (train[s] * value).reshape(-1, 8, train.shape[2])
                 partial[s, pl.ds(pl.multiple_of(place, 8), 8)] = jnp.sum(product, axis=0)
             slot += 1
-    ones = jnp.ones((8, train.shape[2]), jnp.float32)
-    for s in range(train.shape[0]):
-        by_query = jnp.sum(partial[s].reshape(-1, 8, train.shape[2]), axis=1)
-        out[pl.ds(s, 1)] = dot(ones, by_query, NT)[:1]
+    sequences, _, lanes = partial.shape
+    queries = out.shape[1]
+    by_query = jnp.sum(partial[...].reshape(sequences * queries, 8, lanes), axis=1)
+    sums = dot(jnp.ones((8, lanes), jnp.float32), by_query, NT)
+    for s in range(sequences):
+        out[pl.ds(s, 1)] = sums[:1, s * queries : (s + 1) * queries]
 
 
 def exchange(x, devices, distance):

time: 31.5 us -> 31.5 us (level)
  no operation moved by 1% of the time
where the time goes in v2:
time: 31.5 us; the launch traced here: 31.4 us
  starting transfers between devices  15.2 us (48%)
  Pallas kernels  10.3 us (33%)
  waiting for transfers between devices  5.05 us (16%)
  between operations  0.76 us (2%)
    ppermute x13, starting transfers between devices, exchange(): return lax.ppermute(x, 'dp', [(i, i ^ distance) for i in range(devices)])  15.2 us
    pallas_call x1, Pallas kernels, per_device(): pl.pallas_call(functools.partial(front_kernel, tokens * devices, sequence...  6.67 us
    ppermute x13, waiting for transfers between devices, exchange(): return lax.ppermute(x, 'dp', [(i, i ^ distance) for i in range(devices)])  5.05 us
    pallas_call x1, Pallas kernels, per_device(): pl.pallas_call(functools.partial(invert_kernel, sequences, width), out_sh...  2.53 us
    pallas_call x1, Pallas kernels, per_device(): pl.pallas_call(functools.partial(score_kernel, offsets, own_queries), out...  1.08 us
  transfers between devices with their start and end apart: 13, of which 4 were waited for; matrix products, arithmetic and copies ran while one was open for 0% of the time, Pallas kernels for 8%

profile of v2, /device:TPU:0, one launch (start us, length us, event | category | flops | bytes accessed | tf_op | source)
XLA Modules:
  0.0 31.4 jit_solution(13043193376512278926)
XLA Ops:
  0.7 6.7 %front.1 = (f32[72,128]{1,0:T(8,128)S(1)}, f32[4,64,256]{2,1,0:T(8,128)S(1)}, f32[1,96,128]{2,1,0:T(8,128)S(1)}) custom-call(s32[1]{0:T(128)S(6)} %copy.16.ids, bf16[512,4096]{1,0:T(8,128)(2,1)} %acts.1, bf16[512,4096]{1,0:T(8,128)(2,1)} %grad_q.1, bf16[512,1024]{1,0:T(8,128)(2,1)} %grad_k.1, bf16[512,1024]{1,0:T(8,128)(2,1)} %grad_v.1, ...), custom_call_target="tpu_custom_call" | custom-call | tf_op jit(solution)/shard_map/front/pallas_call | solution.py:253
  7.3 0.5 %collective-permute-start = (f32[72,128]{1,0:T(8,128)S(1)}, f32[72,128]{1,0:T(8,128)S(1)}, u32[]{:S(2)}, u32[]{:S(2)}) collective-permute-start(f32[72,128]{1,0:T(8,128)S(1)} %get-tuple-element.17), channel_id=1, source_target_pairs={{0,1},{1,0},{2,3},{3,2},{4,5},{5,4},{6,7},{7,6},{8,9},{9,8},{10,11... | collective-permute-start | bytes 110600 | tf_op jit(solution)/shard_map/ppermute | solution.py:235
  7.9 3.7 %collective-permute-start.4 = (f32[1,96,128]{2,1,0:T(8,128)S(1)}, f32[1,96,128]{2,1,0:T(8,128)S(1)}, u32[]{:S(2)}, u32[]{:S(2)}) collective-permute-start(f32[1,96,128]{2,1,0:T(8,128)S(1)} %get-tuple-element.24), channel_id=1, source_target_pairs={{0,8},{1,9},{2,10},{3,11},{4,12},{5,13},{6,14},{7,15},{8,0},{9,1},... | collective-permute-start | bytes 147464 | tf_op jit(solution)/shard_map/ppermute | solution.py:235
  11.5 0.0 collective-permute-done
  11.5 1.6 %collective-permute-start.1 = (f32[72,128]{1,0:T(8,128)S(1)}, f32[72,128]{1,0:T(8,128)S(1)}, u32[]{:S(2)}, u32[]{:S(2)}) collective-permute-start(f32[72,128]{1,0:T(8,128)S(1)} %add.9), channel_id=1, source_target_pairs={{0,2},{1,3},{2,0},{3,1},{4,6},{5,7},{6,4},{7,5},{8,10},{9,11},{10,... | collective-permute-start | bytes 110600 | tf_op jit(solution)/shard_map/ppermute | solution.py:235
  13.1 0.5 %collective-permute-start.11 = (f32[1,96,128]{2,1,0:T(8,128)S(1)}, f32[1,96,128]{2,1,0:T(8,128)S(1)}, u32[]{:S(2)}, u32[]{:S(2)}) collective-permute-start(f32[1,96,128]{2,1,0:T(8,128)S(1)} %get-tuple-element.24), channel_id=1, source_target_pairs={{0,2},{1,3},{2,0},{3,1},{4,6},{5,7},{6,4},{7,5},{8,10},{9,11},{10,... | collective-permute-start | bytes 147464 | tf_op jit(solution)/shard_map/ppermute | solution.py:235
  13.6 1.9 %collective-permute-done.1 = f32[72,128]{1,0:T(8,128)S(1)} collective-permute-done((f32[72,128]{1,0:T(8,128)S(1)}, f32[72,128]{1,0:T(8,128)S(1)}, u32[]{:S(2)}, u32[]{:S(2)}) %collective-permute-start.1) | collective-permute-done | bytes 36896 | tf_op jit(solution)/shard_map/ppermute | solution.py:235
  15.6 1.6 %collective-permute-start.2 = (f32[72,128]{1,0:T(8,128)S(1)}, f32[72,128]{1,0:T(8,128)S(1)}, u32[]{:S(2)}, u32[]{:S(2)}) collective-permute-start(f32[72,128]{1,0:T(8,128)S(1)} %add.10), channel_id=1, source_target_pairs={{0,4},{1,5},{2,6},{3,7},{4,0},{5,1},{6,2},{7,3},{8,12},{9,13},{10,... | collective-permute-start | bytes 110600 | tf_op jit(solution)/shard_map/ppermute | solution.py:235
  17.1 0.0 collective-permute-done.4
  17.1 1.6 %collective-permute-start.8 = (f32[1,96,128]{2,1,0:T(8,128)S(1)}, f32[1,96,128]{2,1,0:T(8,128)S(1)}, u32[]{:S(2)}, u32[]{:S(2)}) collective-permute-start(f32[1,96,128]{2,1,0:T(8,128)S(1)} %collective-permute-done.4), channel_id=1, source_target_pairs={{0,2},{1,3},{2,0},{3,1},{4,6},{5,7},{6,4},{7,5},{8,10},{9,11},{10,... | collective-permute-start | bytes 147464 | tf_op jit(solution)/shard_map/ppermute | solution.py:235
  18.8 0.4 %collective-permute-start.6 = (f32[1,96,128]{2,1,0:T(8,128)S(1)}, f32[1,96,128]{2,1,0:T(8,128)S(1)}, u32[]{:S(2)}, u32[]{:S(2)}) collective-permute-start(f32[1,96,128]{2,1,0:T(8,128)S(1)} %collective-permute-done.4), channel_id=1, source_target_pairs={{0,4},{1,5},{2,6},{3,7},{4,0},{5,1},{6,2},{7,3},{8,12},{9,13},{10,... | collective-permute-start | bytes 147464 | tf_op jit(solution)/shard_map/ppermute | solution.py:235
  19.2 1.6 %collective-permute-start.5 = (f32[1,96,128]{2,1,0:T(8,128)S(1)}, f32[1,96,128]{2,1,0:T(8,128)S(1)}, u32[]{:S(2)}, u32[]{:S(2)}) collective-permute-start(f32[1,96,128]{2,1,0:T(8,128)S(1)} %get-tuple-element.24), channel_id=1, source_target_pairs={{0,4},{1,5},{2,6},{3,7},{4,0},{5,1},{6,2},{7,3},{8,12},{9,13},{10,... | collective-permute-start | bytes 147464 | tf_op jit(solution)/shard_map/ppermute | solution.py:235
  20.8 0.0 collective-permute-done.2
  20.8 1.1 %collective-permute-start.3 = (f32[72,128]{1,0:T(8,128)S(1)}, f32[72,128]{1,0:T(8,128)S(1)}, u32[]{:S(2)}, u32[]{:S(2)}) collective-permute-start(f32[72,128]{1,0:T(8,128)S(1)} %add.11.first), channel_id=1, source_target_pairs={{0,8},{1,9},{2,10},{3,11},{4,12},{5,13},{6,14},{7,15},{8,0},{9,1},... | collective-permute-start | bytes 110600 | tf_op jit(solution)/shard_map/ppermute | solution.py:235
  21.9 1.7 %collective-permute-done.5 = f32[1,96,128]{2,1,0:T(8,128)S(1)} collective-permute-done((f32[1,96,128]{2,1,0:T(8,128)S(1)}, f32[1,96,128]{2,1,0:T(8,128)S(1)}, u32[]{:S(2)}, u32[]{:S(2)}) %collective-permute-start.5) | collective-permute-done | bytes 49184 | tf_op jit(solution)/shard_map/ppermute | solution.py:235
  23.6 0.0 collective-permute-done.6
  23.6 0.5 %collective-permute-start.9 = (f32[1,96,128]{2,1,0:T(8,128)S(1)}, f32[1,96,128]{2,1,0:T(8,128)S(1)}, u32[]{:S(2)}, u32[]{:S(2)}) collective-permute-start(f32[1,96,128]{2,1,0:T(8,128)S(1)} %collective-permute-done.5), channel_id=1, source_target_pairs={{0,2},{1,3},{2,0},{3,1},{4,6},{5,7},{6,4},{7,5},{8,10},{9,11},{10,... | collective-permute-start | bytes 147464 | tf_op jit(solution)/shard_map/ppermute | solution.py:235
  24.1 1.5 %collective-permute-start.10 = (f32[1,96,128]{2,1,0:T(8,128)S(1)}, f32[1,96,128]{2,1,0:T(8,128)S(1)}, u32[]{:S(2)}, u32[]{:S(2)}) collective-permute-start(f32[1,96,128]{2,1,0:T(8,128)S(1)} %collective-permute-done.6), channel_id=1, source_target_pairs={{0,2},{1,3},{2,0},{3,1},{4,6},{5,7},{6,4},{7,5},{8,10},{9,11},{10,... | collective-permute-start | bytes 147464 | tf_op jit(solution)/shard_map/ppermute | solution.py:235
  25.7 0.4 %collective-permute-done.3.second = f32[72,128]{1,0:T(8,128)S(1)} collective-permute-done((f32[72,128]{1,0:T(8,128)S(1)}, f32[72,128]{1,0:T(8,128)S(1)}, u32[]{:S(2)}, u32[]{:S(2)}) %collective-permute-start.3) | collective-permute-done | bytes 36896 | tf_op jit(solution)/shard_map/ppermute | solution.py:235
  26.0 0.0 collective-permute-start.7
  26.0 2.5 %invert.1.train = f32[4,96,128]{2,1,0:T(8,128)S(1)} custom-call(f32[72,128]{1,0:T(8,128)S(1)} %add.11.first, f32[72,128]{1,0:T(8,128)S(1)} %collective-permute-done.3.second, f32[4,64,256]{2,1,0:T(8,128)S(1)} %get-tuple-element.18.grams), custom_call_target="tpu_custom_call" | custom-call | tf_op jit(solution)/shard_map/invert/pallas_call | solution.py:307
  28.6 0.0 collective-permute-done.11
  28.6 0.0 collective-permute-done.8
  28.6 0.0 collective-permute-done.9
  28.6 0.0 collective-permute-done.10
  28.7 0.6 %collective-permute-start.12 = (f32[4,96,128]{2,1,0:T(8,128)S(1)}, f32[4,96,128]{2,1,0:T(8,128)S(1)}, u32[]{:S(2)}, u32[]{:S(2)}) collective-permute-start(f32[4,96,128]{2,1,0:T(8,128)S(1)} %constant_dynamic-update-slice_fusion.4.refs_2_), channel_id=1, source_target_pairs={{0,1},{1,0},{2,3},{3,2},{4,5},{5,4},{6,7},{7,6},{8,9},{9,8},{10,11... | collective-permute-start | bytes 589832 | tf_op jit(solution)/shard_map/ppermute | solution.py:235
  29.2 0.0 collective-permute-done.7.refs_1_
  29.2 1.1 %collective-permute-done.12.refs_3_ = f32[4,96,128]{2,1,0:T(8,128)S(1)} collective-permute-done((f32[4,96,128]{2,1,0:T(8,128)S(1)}, f32[4,96,128]{2,1,0:T(8,128)S(1)}, u32[]{:S(2)}, u32[]{:S(2)}) %collective-permute-start.12) | collective-permute-done | bytes 196640 | tf_op jit(solution)/shard_map/ppermute | solution.py:235
  30.3 1.1 %scores.1 = f32[4,16]{1,0:T(4,128)} custom-call(f32[4,96,128]{2,1,0:T(8,128)S(1)} %invert.1.train, f32[4,96,128]{2,1,0:T(8,128)S(1)} %constant_dynamic-update-slice_fusion.refs_0_, f32[4,96,128]{2,1,0:T(8,128)S(1)} %collective-permute-done.7.refs_1_, f32[4,96,128]{2,1,0:T(8,128)S(1)} %constant_dynamic-update-slice_fusion.4.refs_2_, ...), custom_call_target="tpu_custom_call" | custom-call | tf_op jit(solution)/shard_map/scores/pallas_call | solution.py:323
  (11 shorter events, 0.1 us)
Async XLA Ops:
  7.3 4.2 %collective-permute-start = (f32[72,128]{1,0:T(8,128)S(1)}, f32[72,128]{1,0:T(8,128)S(1)}, u32[]{:S(2)}, u32[]{:S(2)}) collective-permute-start(f32[72,128]{1,0:T(8,128)S(1)} %get-tuple-element.17), channel_id=1, source_target_pairs={{0,1},{1,0},{2,3},{3,2},{4,5},{5,4},{6,7},{7,6},{8,9},{9,8},{10,11... | collective-permute-start | bytes 110600 | tf_op jit(solution)/shard_map/ppermute | solution.py:235
  7.9 9.3 %collective-permute-start.4 = (f32[1,96,128]{2,1,0:T(8,128)S(1)}, f32[1,96,128]{2,1,0:T(8,128)S(1)}, u32[]{:S(2)}, u32[]{:S(2)}) collective-permute-start(f32[1,96,128]{2,1,0:T(8,128)S(1)} %get-tuple-element.24), channel_id=1, source_target_pairs={{0,8},{1,9},{2,10},{3,11},{4,12},{5,13},{6,14},{7,15},{8,0},{9,1},... | collective-permute-start | bytes 147464 | tf_op jit(solution)/shard_map/ppermute | solution.py:235
  11.5 4.0 %collective-permute-start.1 = (f32[72,128]{1,0:T(8,128)S(1)}, f32[72,128]{1,0:T(8,128)S(1)}, u32[]{:S(2)}, u32[]{:S(2)}) collective-permute-start(f32[72,128]{1,0:T(8,128)S(1)} %add.9), channel_id=1, source_target_pairs={{0,2},{1,3},{2,0},{3,1},{4,6},{5,7},{6,4},{7,5},{8,10},{9,11},{10,... | collective-permute-start | bytes 110600 | tf_op jit(solution)/shard_map/ppermute | solution.py:235
  13.1 15.5 %collective-permute-start.11 = (f32[1,96,128]{2,1,0:T(8,128)S(1)}, f32[1,96,128]{2,1,0:T(8,128)S(1)}, u32[]{:S(2)}, u32[]{:S(2)}) collective-permute-start(f32[1,96,128]{2,1,0:T(8,128)S(1)} %get-tuple-element.24), channel_id=1, source_target_pairs={{0,2},{1,3},{2,0},{3,1},{4,6},{5,7},{6,4},{7,5},{8,10},{9,11},{10,... | collective-permute-start | bytes 147464 | tf_op jit(solution)/shard_map/ppermute | solution.py:235
  15.6 5.3 %collective-permute-start.2 = (f32[72,128]{1,0:T(8,128)S(1)}, f32[72,128]{1,0:T(8,128)S(1)}, u32[]{:S(2)}, u32[]{:S(2)}) collective-permute-start(f32[72,128]{1,0:T(8,128)S(1)} %add.10), channel_id=1, source_target_pairs={{0,4},{1,5},{2,6},{3,7},{4,0},{5,1},{6,2},{7,3},{8,12},{9,13},{10,... | collective-permute-start | bytes 110600 | tf_op jit(solution)/shard_map/ppermute | solution.py:235
  17.1 11.5 %collective-permute-start.8 = (f32[1,96,128]{2,1,0:T(8,128)S(1)}, f32[1,96,128]{2,1,0:T(8,128)S(1)}, u32[]{:S(2)}, u32[]{:S(2)}) collective-permute-start(f32[1,96,128]{2,1,0:T(8,128)S(1)} %collective-permute-done.4), channel_id=1, source_target_pairs={{0,2},{1,3},{2,0},{3,1},{4,6},{5,7},{6,4},{7,5},{8,10},{9,11},{10,... | collective-permute-start | bytes 147464 | tf_op jit(solution)/shard_map/ppermute | solution.py:235
  18.8 4.8 %collective-permute-start.6 = (f32[1,96,128]{2,1,0:T(8,128)S(1)}, f32[1,96,128]{2,1,0:T(8,128)S(1)}, u32[]{:S(2)}, u32[]{:S(2)}) collective-permute-start(f32[1,96,128]{2,1,0:T(8,128)S(1)} %collective-permute-done.4), channel_id=1, source_target_pairs={{0,4},{1,5},{2,6},{3,7},{4,0},{5,1},{6,2},{7,3},{8,12},{9,13},{10,... | collective-permute-start | bytes 147464 | tf_op jit(solution)/shard_map/ppermute | solution.py:235
  19.2 4.4 %collective-permute-start.5 = (f32[1,96,128]{2,1,0:T(8,128)S(1)}, f32[1,96,128]{2,1,0:T(8,128)S(1)}, u32[]{:S(2)}, u32[]{:S(2)}) collective-permute-start(f32[1,96,128]{2,1,0:T(8,128)S(1)} %get-tuple-element.24), channel_id=1, source_target_pairs={{0,4},{1,5},{2,6},{3,7},{4,0},{5,1},{6,2},{7,3},{8,12},{9,13},{10,... | collective-permute-start | bytes 147464 | tf_op jit(solution)/shard_map/ppermute | solution.py:235
  20.8 5.2 %collective-permute-start.3 = (f32[72,128]{1,0:T(8,128)S(1)}, f32[72,128]{1,0:T(8,128)S(1)}, u32[]{:S(2)}, u32[]{:S(2)}) collective-permute-start(f32[72,128]{1,0:T(8,128)S(1)} %add.11.first), channel_id=1, source_target_pairs={{0,8},{1,9},{2,10},{3,11},{4,12},{5,13},{6,14},{7,15},{8,0},{9,1},... | collective-permute-start | bytes 110600 | tf_op jit(solution)/shard_map/ppermute | solution.py:235
  23.6 5.0 %collective-permute-start.9 = (f32[1,96,128]{2,1,0:T(8,128)S(1)}, f32[1,96,128]{2,1,0:T(8,128)S(1)}, u32[]{:S(2)}, u32[]{:S(2)}) collective-permute-start(f32[1,96,128]{2,1,0:T(8,128)S(1)} %collective-permute-done.5), channel_id=1, source_target_pairs={{0,2},{1,3},{2,0},{3,1},{4,6},{5,7},{6,4},{7,5},{8,10},{9,11},{10,... | collective-permute-start | bytes 147464 | tf_op jit(solution)/shard_map/ppermute | solution.py:235
  24.1 4.5 %collective-permute-start.10 = (f32[1,96,128]{2,1,0:T(8,128)S(1)}, f32[1,96,128]{2,1,0:T(8,128)S(1)}, u32[]{:S(2)}, u32[]{:S(2)}) collective-permute-start(f32[1,96,128]{2,1,0:T(8,128)S(1)} %collective-permute-done.6), channel_id=1, source_target_pairs={{0,2},{1,3},{2,0},{3,1},{4,6},{5,7},{6,4},{7,5},{8,10},{9,11},{10,... | collective-permute-start | bytes 147464 | tf_op jit(solution)/shard_map/ppermute | solution.py:235
  26.0 3.2 %collective-permute-start.7 = (f32[4,96,128]{2,1,0:T(8,128)S(1)}, f32[4,96,128]{2,1,0:T(8,128)S(1)}, u32[]{:S(2)}, u32[]{:S(2)}) collective-permute-start(f32[4,96,128]{2,1,0:T(8,128)S(1)} %constant_dynamic-update-slice_fusion.refs_0_), channel_id=1, source_target_pairs={{0,1},{1,0},{2,3},{3,2},{4,5},{5,4},{6,7},{7,6},{8,9},{9,8},{10,11... | collective-permute-start | bytes 589832 | tf_op jit(solution)/shard_map/ppermute | solution.py:235
  28.7 1.6 %collective-permute-start.12 = (f32[4,96,128]{2,1,0:T(8,128)S(1)}, f32[4,96,128]{2,1,0:T(8,128)S(1)}, u32[]{:S(2)}, u32[]{:S(2)}) collective-permute-start(f32[4,96,128]{2,1,0:T(8,128)S(1)} %constant_dynamic-update-slice_fusion.4.refs_2_), channel_id=1, source_target_pairs={{0,1},{1,0},{2,3},{3,2},{4,5},{5,4},{6,7},{7,6},{8,9},{9,8},{10,11... | collective-permute-start | bytes 589832 | tf_op jit(solution)/shard_map/ppermute | solution.py:235

commit v3 on v1

--- a/solution.py
+++ b/solution.py
@@ -11,7 +11,7 @@
 LANES = 128
 PANEL = 8
 HALF = 128
-IN_FLIGHT = 6
+IN_FLIGHT = 12
 MESSAGES = 4
 HIGHEST = lax.Precision.HIGHEST
 FRONT_VMEM_BYTES = 24 * 1024 * 1024

time: 31.5 us -> 31.4 us (level)
  no operation moved by 1% of the time
where the time goes in v3:
time: 31.4 us; the launch traced here: 31.2 us
  starting transfers between devices  15.2 us (48%)
  Pallas kernels  10.1 us (32%)
  waiting for transfers between devices  5.05 us (16%)
  between operations  0.76 us (2%)
    ppermute x13, starting transfers between devices, exchange(): return lax.ppermute(x, 'dp', [(i, i ^ distance) for i in range(devices)])  15.2 us
    pallas_call x1, Pallas kernels, per_device(): pl.pallas_call(functools.partial(front_kernel, tokens * devices, sequence...  6.55 us
    ppermute x13, waiting for transfers between devices, exchange(): return lax.ppermute(x, 'dp', [(i, i ^ distance) for i in range(devices)])  5.05 us
    pallas_call x1, Pallas kernels, per_device(): pl.pallas_call(functools.partial(invert_kernel, sequences, width), out_sh...  2.53 us
    pallas_call x1, Pallas kernels, per_device(): pl.pallas_call(functools.partial(score_kernel, offsets, own_queries), out...  1.02 us
  transfers between devices with their start and end apart: 13, of which 4 were waited for; matrix products, arithmetic and copies ran while one was open for 0% of the time, Pallas kernels for 8%

profile of v3, /device:TPU:0, one launch (start us, length us, event | category | flops | bytes accessed | tf_op | source)
XLA Modules:
  0.0 31.2 jit_solution(12268273348971268415)
XLA Ops:
  0.7 6.5 %front.1 = (f32[72,128]{1,0:T(8,128)S(1)}, f32[4,64,256]{2,1,0:T(8,128)S(1)}, f32[1,96,128]{2,1,0:T(8,128)S(1)}) custom-call(s32[1]{0:T(128)S(6)} %copy.16.ids, bf16[512,4096]{1,0:T(8,128)(2,1)} %acts.1, bf16[512,4096]{1,0:T(8,128)(2,1)} %grad_q.1, bf16[512,1024]{1,0:T(8,128)(2,1)} %grad_k.1, bf16[512,1024]{1,0:T(8,128)(2,1)} %grad_v.1, ...), custom_call_target="tpu_custom_call" | custom-call | tf_op jit(solution)/shard_map/front/pallas_call | solution.py:251
  7.2 0.5 %collective-permute-start = (f32[72,128]{1,0:T(8,128)S(1)}, f32[72,128]{1,0:T(8,128)S(1)}, u32[]{:S(2)}, u32[]{:S(2)}) collective-permute-start(f32[72,128]{1,0:T(8,128)S(1)} %get-tuple-element.17), channel_id=1, source_target_pairs={{0,1},{1,0},{2,3},{3,2},{4,5},{5,4},{6,7},{7,6},{8,9},{9,8},{10,11... | collective-permute-start | bytes 110600 | tf_op jit(solution)/shard_map/ppermute | solution.py:233
  7.7 3.7 %collective-permute-start.4 = (f32[1,96,128]{2,1,0:T(8,128)S(1)}, f32[1,96,128]{2,1,0:T(8,128)S(1)}, u32[]{:S(2)}, u32[]{:S(2)}) collective-permute-start(f32[1,96,128]{2,1,0:T(8,128)S(1)} %get-tuple-element.24), channel_id=1, source_target_pairs={{0,8},{1,9},{2,10},{3,11},{4,12},{5,13},{6,14},{7,15},{8,0},{9,1},... | collective-permute-start | bytes 147464 | tf_op jit(solution)/shard_map/ppermute | solution.py:233
  11.4 0.0 collective-permute-done
  11.4 1.6 %collective-permute-start.1 = (f32[72,128]{1,0:T(8,128)S(1)}, f32[72,128]{1,0:T(8,128)S(1)}, u32[]{:S(2)}, u32[]{:S(2)}) collective-permute-start(f32[72,128]{1,0:T(8,128)S(1)} %add.9), channel_id=1, source_target_pairs={{0,2},{1,3},{2,0},{3,1},{4,6},{5,7},{6,4},{7,5},{8,10},{9,11},{10,... | collective-permute-start | bytes 110600 | tf_op jit(solution)/shard_map/ppermute | solution.py:233
  13.0 0.5 %collective-permute-start.11 = (f32[1,96,128]{2,1,0:T(8,128)S(1)}, f32[1,96,128]{2,1,0:T(8,128)S(1)}, u32[]{:S(2)}, u32[]{:S(2)}) collective-permute-start(f32[1,96,128]{2,1,0:T(8,128)S(1)} %get-tuple-element.24), channel_id=1, source_target_pairs={{0,2},{1,3},{2,0},{3,1},{4,6},{5,7},{6,4},{7,5},{8,10},{9,11},{10,... | collective-permute-start | bytes 147464 | tf_op jit(solution)/shard_map/ppermute | solution.py:233
  13.5 1.9 %collective-permute-done.1 = f32[72,128]{1,0:T(8,128)S(1)} collective-permute-done((f32[72,128]{1,0:T(8,128)S(1)}, f32[72,128]{1,0:T(8,128)S(1)}, u32[]{:S(2)}, u32[]{:S(2)}) %collective-permute-start.1) | collective-permute-done | bytes 36896 | tf_op jit(solution)/shard_map/ppermute | solution.py:233
  15.4 1.6 %collective-permute-start.2 = (f32[72,128]{1,0:T(8,128)S(1)}, f32[72,128]{1,0:T(8,128)S(1)}, u32[]{:S(2)}, u32[]{:S(2)}) collective-permute-start(f32[72,128]{1,0:T(8,128)S(1)} %add.10), channel_id=1, source_target_pairs={{0,4},{1,5},{2,6},{3,7},{4,0},{5,1},{6,2},{7,3},{8,12},{9,13},{10,... | collective-permute-start | bytes 110600 | tf_op jit(solution)/shard_map/ppermute | solution.py:233
  17.0 0.0 collective-permute-done.4
  17.0 1.6 %collective-permute-start.8 = (f32[1,96,128]{2,1,0:T(8,128)S(1)}, f32[1,96,128]{2,1,0:T(8,128)S(1)}, u32[]{:S(2)}, u32[]{:S(2)}) collective-permute-start(f32[1,96,128]{2,1,0:T(8,128)S(1)} %collective-permute-done.4), channel_id=1, source_target_pairs={{0,2},{1,3},{2,0},{3,1},{4,6},{5,7},{6,4},{7,5},{8,10},{9,11},{10,... | collective-permute-start | bytes 147464 | tf_op jit(solution)/shard_map/ppermute | solution.py:233
  18.7 0.4 %collective-permute-start.6 = (f32[1,96,128]{2,1,0:T(8,128)S(1)}, f32[1,96,128]{2,1,0:T(8,128)S(1)}, u32[]{:S(2)}, u32[]{:S(2)}) collective-permute-start(f32[1,96,128]{2,1,0:T(8,128)S(1)} %collective-permute-done.4), channel_id=1, source_target_pairs={{0,4},{1,5},{2,6},{3,7},{4,0},{5,1},{6,2},{7,3},{8,12},{9,13},{10,... | collective-permute-start | bytes 147464 | tf_op jit(solution)/shard_map/ppermute | solution.py:233
  19.1 1.6 %collective-permute-start.5 = (f32[1,96,128]{2,1,0:T(8,128)S(1)}, f32[1,96,128]{2,1,0:T(8,128)S(1)}, u32[]{:S(2)}, u32[]{:S(2)}) collective-permute-start(f32[1,96,128]{2,1,0:T(8,128)S(1)} %get-tuple-element.24), channel_id=1, source_target_pairs={{0,4},{1,5},{2,6},{3,7},{4,0},{5,1},{6,2},{7,3},{8,12},{9,13},{10,... | collective-permute-start | bytes 147464 | tf_op jit(solution)/shard_map/ppermute | solution.py:233
  20.7 0.0 collective-permute-done.2
  20.7 1.1 %collective-permute-start.3 = (f32[72,128]{1,0:T(8,128)S(1)}, f32[72,128]{1,0:T(8,128)S(1)}, u32[]{:S(2)}, u32[]{:S(2)}) collective-permute-start(f32[72,128]{1,0:T(8,128)S(1)} %add.11.first), channel_id=1, source_target_pairs={{0,8},{1,9},{2,10},{3,11},{4,12},{5,13},{6,14},{7,15},{8,0},{9,1},... | collective-permute-start | bytes 110600 | tf_op jit(solution)/shard_map/ppermute | solution.py:233
  21.8 1.7 %collective-permute-done.5 = f32[1,96,128]{2,1,0:T(8,128)S(1)} collective-permute-done((f32[1,96,128]{2,1,0:T(8,128)S(1)}, f32[1,96,128]{2,1,0:T(8,128)S(1)}, u32[]{:S(2)}, u32[]{:S(2)}) %collective-permute-start.5) | collective-permute-done | bytes 49184 | tf_op jit(solution)/shard_map/ppermute | solution.py:233
  23.5 0.0 collective-permute-done.6
  23.5 0.5 %collective-permute-start.9 = (f32[1,96,128]{2,1,0:T(8,128)S(1)}, f32[1,96,128]{2,1,0:T(8,128)S(1)}, u32[]{:S(2)}, u32[]{:S(2)}) collective-permute-start(f32[1,96,128]{2,1,0:T(8,128)S(1)} %collective-permute-done.5), channel_id=1, source_target_pairs={{0,2},{1,3},{2,0},{3,1},{4,6},{5,7},{6,4},{7,5},{8,10},{9,11},{10,... | collective-permute-start | bytes 147464 | tf_op jit(solution)/shard_map/ppermute | solution.py:233
  24.0 1.5 %collective-permute-start.10 = (f32[1,96,128]{2,1,0:T(8,128)S(1)}, f32[1,96,128]{2,1,0:T(8,128)S(1)}, u32[]{:S(2)}, u32[]{:S(2)}) collective-permute-start(f32[1,96,128]{2,1,0:T(8,128)S(1)} %collective-permute-done.6), channel_id=1, source_target_pairs={{0,2},{1,3},{2,0},{3,1},{4,6},{5,7},{6,4},{7,5},{8,10},{9,11},{10,... | collective-permute-start | bytes 147464 | tf_op jit(solution)/shard_map/ppermute | solution.py:233
  25.5 0.4 %collective-permute-done.3.second = f32[72,128]{1,0:T(8,128)S(1)} collective-permute-done((f32[72,128]{1,0:T(8,128)S(1)}, f32[72,128]{1,0:T(8,128)S(1)}, u32[]{:S(2)}, u32[]{:S(2)}) %collective-permute-start.3) | collective-permute-done | bytes 36896 | tf_op jit(solution)/shard_map/ppermute | solution.py:233
  25.9 0.0 collective-permute-start.7
  25.9 2.5 %invert.1.train = f32[4,96,128]{2,1,0:T(8,128)S(1)} custom-call(f32[72,128]{1,0:T(8,128)S(1)} %add.11.first, f32[72,128]{1,0:T(8,128)S(1)} %collective-permute-done.3.second, f32[4,64,256]{2,1,0:T(8,128)S(1)} %get-tuple-element.18.grams), custom_call_target="tpu_custom_call" | custom-call | tf_op jit(solution)/shard_map/invert/pallas_call | solution.py:305
  28.5 0.0 collective-permute-done.11
  28.5 0.0 collective-permute-done.8
  28.5 0.0 collective-permute-done.9
  28.5 0.0 collective-permute-done.10
  28.6 0.6 %collective-permute-start.12 = (f32[4,96,128]{2,1,0:T(8,128)S(1)}, f32[4,96,128]{2,1,0:T(8,128)S(1)}, u32[]{:S(2)}, u32[]{:S(2)}) collective-permute-start(f32[4,96,128]{2,1,0:T(8,128)S(1)} %constant_dynamic-update-slice_fusion.4.refs_2_), channel_id=1, source_target_pairs={{0,1},{1,0},{2,3},{3,2},{4,5},{5,4},{6,7},{7,6},{8,9},{9,8},{10,11... | collective-permute-start | bytes 589832 | tf_op jit(solution)/shard_map/ppermute | solution.py:233
  29.1 0.0 collective-permute-done.7.refs_1_
  29.1 1.1 %collective-permute-done.12.refs_3_ = f32[4,96,128]{2,1,0:T(8,128)S(1)} collective-permute-done((f32[4,96,128]{2,1,0:T(8,128)S(1)}, f32[4,96,128]{2,1,0:T(8,128)S(1)}, u32[]{:S(2)}, u32[]{:S(2)}) %collective-permute-start.12) | collective-permute-done | bytes 196640 | tf_op jit(solution)/shard_map/ppermute | solution.py:233
  30.2 1.0 %scores.1 = f32[4,16]{1,0:T(4,128)} custom-call(f32[4,96,128]{2,1,0:T(8,128)S(1)} %invert.1.train, f32[4,96,128]{2,1,0:T(8,128)S(1)} %constant_dynamic-update-slice_fusion.refs_0_, f32[4,96,128]{2,1,0:T(8,128)S(1)} %collective-permute-done.7.refs_1_, f32[4,96,128]{2,1,0:T(8,128)S(1)} %constant_dynamic-update-slice_fusion.4.refs_2_, ...), custom_call_target="tpu_custom_call" | custom-call | tf_op jit(solution)/shard_map/scores/pallas_call | solution.py:321
  (11 shorter events, 0.1 us)
Async XLA Ops:
  7.2 4.2 %collective-permute-start = (f32[72,128]{1,0:T(8,128)S(1)}, f32[72,128]{1,0:T(8,128)S(1)}, u32[]{:S(2)}, u32[]{:S(2)}) collective-permute-start(f32[72,128]{1,0:T(8,128)S(1)} %get-tuple-element.17), channel_id=1, source_target_pairs={{0,1},{1,0},{2,3},{3,2},{4,5},{5,4},{6,7},{7,6},{8,9},{9,8},{10,11... | collective-permute-start | bytes 110600 | tf_op jit(solution)/shard_map/ppermute | solution.py:233
  7.7 9.3 %collective-permute-start.4 = (f32[1,96,128]{2,1,0:T(8,128)S(1)}, f32[1,96,128]{2,1,0:T(8,128)S(1)}, u32[]{:S(2)}, u32[]{:S(2)}) collective-permute-start(f32[1,96,128]{2,1,0:T(8,128)S(1)} %get-tuple-element.24), channel_id=1, source_target_pairs={{0,8},{1,9},{2,10},{3,11},{4,12},{5,13},{6,14},{7,15},{8,0},{9,1},... | collective-permute-start | bytes 147464 | tf_op jit(solution)/shard_map/ppermute | solution.py:233
  11.4 4.0 %collective-permute-start.1 = (f32[72,128]{1,0:T(8,128)S(1)}, f32[72,128]{1,0:T(8,128)S(1)}, u32[]{:S(2)}, u32[]{:S(2)}) collective-permute-start(f32[72,128]{1,0:T(8,128)S(1)} %add.9), channel_id=1, source_target_pairs={{0,2},{1,3},{2,0},{3,1},{4,6},{5,7},{6,4},{7,5},{8,10},{9,11},{10,... | collective-permute-start | bytes 110600 | tf_op jit(solution)/shard_map/ppermute | solution.py:233
  13.0 15.5 %collective-permute-start.11 = (f32[1,96,128]{2,1,0:T(8,128)S(1)}, f32[1,96,128]{2,1,0:T(8,128)S(1)}, u32[]{:S(2)}, u32[]{:S(2)}) collective-permute-start(f32[1,96,128]{2,1,0:T(8,128)S(1)} %get-tuple-element.24), channel_id=1, source_target_pairs={{0,2},{1,3},{2,0},{3,1},{4,6},{5,7},{6,4},{7,5},{8,10},{9,11},{10,... | collective-permute-start | bytes 147464 | tf_op jit(solution)/shard_map/ppermute | solution.py:233
  15.4 5.3 %collective-permute-start.2 = (f32[72,128]{1,0:T(8,128)S(1)}, f32[72,128]{1,0:T(8,128)S(1)}, u32[]{:S(2)}, u32[]{:S(2)}) collective-permute-start(f32[72,128]{1,0:T(8,128)S(1)} %add.10), channel_id=1, source_target_pairs={{0,4},{1,5},{2,6},{3,7},{4,0},{5,1},{6,2},{7,3},{8,12},{9,13},{10,... | collective-permute-start | bytes 110600 | tf_op jit(solution)/shard_map/ppermute | solution.py:233
  17.0 11.5 %collective-permute-start.8 = (f32[1,96,128]{2,1,0:T(8,128)S(1)}, f32[1,96,128]{2,1,0:T(8,128)S(1)}, u32[]{:S(2)}, u32[]{:S(2)}) collective-permute-start(f32[1,96,128]{2,1,0:T(8,128)S(1)} %collective-permute-done.4), channel_id=1, source_target_pairs={{0,2},{1,3},{2,0},{3,1},{4,6},{5,7},{6,4},{7,5},{8,10},{9,11},{10,... | collective-permute-start | bytes 147464 | tf_op jit(solution)/shard_map/ppermute | solution.py:233
  18.7 4.8 %collective-permute-start.6 = (f32[1,96,128]{2,1,0:T(8,128)S(1)}, f32[1,96,128]{2,1,0:T(8,128)S(1)}, u32[]{:S(2)}, u32[]{:S(2)}) collective-permute-start(f32[1,96,128]{2,1,0:T(8,128)S(1)} %collective-permute-done.4), channel_id=1, source_target_pairs={{0,4},{1,5},{2,6},{3,7},{4,0},{5,1},{6,2},{7,3},{8,12},{9,13},{10,... | collective-permute-start | bytes 147464 | tf_op jit(solution)/shard_map/ppermute | solution.py:233
  19.1 4.4 %collective-permute-start.5 = (f32[1,96,128]{2,1,0:T(8,128)S(1)}, f32[1,96,128]{2,1,0:T(8,128)S(1)}, u32[]{:S(2)}, u32[]{:S(2)}) collective-permute-start(f32[1,96,128]{2,1,0:T(8,128)S(1)} %get-tuple-element.24), channel_id=1, source_target_pairs={{0,4},{1,5},{2,6},{3,7},{4,0},{5,1},{6,2},{7,3},{8,12},{9,13},{10,... | collective-permute-start | bytes 147464 | tf_op jit(solution)/shard_map/ppermute | solution.py:233
  20.7 5.2 %collective-permute-start.3 = (f32[72,128]{1,0:T(8,128)S(1)}, f32[72,128]{1,0:T(8,128)S(1)}, u32[]{:S(2)}, u32[]{:S(2)}) collective-permute-start(f32[72,128]{1,0:T(8,128)S(1)} %add.11.first), channel_id=1, source_target_pairs={{0,8},{1,9},{2,10},{3,11},{4,12},{5,13},{6,14},{7,15},{8,0},{9,1},... | collective-permute-start | bytes 110600 | tf_op jit(solution)/shard_map/ppermute | solution.py:233
  23.5 5.0 %collective-permute-start.9 = (f32[1,96,128]{2,1,0:T(8,128)S(1)}, f32[1,96,128]{2,1,0:T(8,128)S(1)}, u32[]{:S(2)}, u32[]{:S(2)}) collective-permute-start(f32[1,96,128]{2,1,0:T(8,128)S(1)} %collective-permute-done.5), channel_id=1, source_target_pairs={{0,2},{1,3},{2,0},{3,1},{4,6},{5,7},{6,4},{7,5},{8,10},{9,11},{10,... | collective-permute-start | bytes 147464 | tf_op jit(solution)/shard_map/ppermute | solution.py:233
  24.0 4.5 %collective-permute-start.10 = (f32[1,96,128]{2,1,0:T(8,128)S(1)}, f32[1,96,128]{2,1,0:T(8,128)S(1)}, u32[]{:S(2)}, u32[]{:S(2)}) collective-permute-start(f32[1,96,128]{2,1,0:T(8,128)S(1)} %collective-permute-done.6), channel_id=1, source_target_pairs={{0,2},{1,3},{2,0},{3,1},{4,6},{5,7},{6,4},{7,5},{8,10},{9,11},{10,... | collective-permute-start | bytes 147464 | tf_op jit(solution)/shard_map/ppermute | solution.py:233
  25.9 3.2 %collective-permute-start.7 = (f32[4,96,128]{2,1,0:T(8,128)S(1)}, f32[4,96,128]{2,1,0:T(8,128)S(1)}, u32[]{:S(2)}, u32[]{:S(2)}) collective-permute-start(f32[4,96,128]{2,1,0:T(8,128)S(1)} %constant_dynamic-update-slice_fusion.refs_0_), channel_id=1, source_target_pairs={{0,1},{1,0},{2,3},{3,2},{4,5},{5,4},{6,7},{7,6},{8,9},{9,8},{10,11... | collective-permute-start | bytes 589832 | tf_op jit(solution)/shard_map/ppermute | solution.py:233
  28.6 1.6 %collective-permute-start.12 = (f32[4,96,128]{2,1,0:T(8,128)S(1)}, f32[4,96,128]{2,1,0:T(8,128)S(1)}, u32[]{:S(2)}, u32[]{:S(2)}) collective-permute-start(f32[4,96,128]{2,1,0:T(8,128)S(1)} %constant_dynamic-update-slice_fusion.4.refs_2_), channel_id=1, source_target_pairs={{0,1},{1,0},{2,3},{3,2},{4,5},{5,4},{6,7},{7,6},{8,9},{9,8},{10,11... | collective-permute-start | bytes 589832 | tf_op jit(solution)/shard_map/ppermute | solution.py:233
